TPU v7x, 32 devices: a whole 2x2x4 slice. The times are simulated.
32 devices in a mesh: row: 4 (over y, x), col: 4 (over z), layer: 2 (over core).
Axes of the slice: x: 2, y: 2, z: 4, core: 2. Of those that a mesh axis runs over, the one named last changes fastest.
Arguments:
- a_tiles: bfloat16 [4, 2, 4, 16, 128, 128], P('row', 'layer', 'col'), may hold values from -6 to 6
- a_place: int32 [4, 2, 4, 16], P('row', 'layer', 'col'), may hold values from 0 to 31, as said below
- a_count: int32 [4, 2, 4], P('row', 'layer', 'col'), may hold values from 8 to 16, as said below
- b_tiles: bfloat16 [2, 4, 4, 64, 128, 128], P('layer', 'row', 'col'), may hold values from -0.09375 to 0.09375
- b_place: int32 [2, 4, 4, 64], P('layer', 'row', 'col'), may hold values from 0 to 127, as said below
- b_count: int32 [2, 4, 4], P('layer', 'row', 'col'), may hold values from 32 to 64, as said below
- out_place: int32 [4, 4, 32], P('row', 'col'), may hold values from 0 to 63, as said below
Outputs:
- out_tiles: bfloat16 [4, 4, 32, 128, 128], P('row', 'col', 'layer')
Inputs may be any that keep to these rules, and one draw needn't show every extreme that they name: `a_place`: the 16 slots of a shard hold distinct positions of its 4 x 8 tile block. `a_count`: some shard uses all its slots. `b_place`: the 64 slots of a shard hold distinct positions of its 8 x 16 tile block. `b_count`: some shard uses all its slots. `out_place`: the 32 positions of a block are distinct positions of its 4 x 16 tile block.
All inputs are finite; a program needn't handle non-finite values.
Results may differ from a plain program's by a relative error of at most 0.001.
Values may be sent and summed in bfloat16 or wider, within the bound.
No kernel may reach another device: no remote copies, remote signals or barrier semaphores. Data moves between devices by JAX's collectives and lax.ppermute only.
A program may use at most 128 MiB of HBM per device.

v0:
```python
import jax
import jax.numpy as jnp
from jax import lax
from jax.sharding import PartitionSpec as P

TB = 4
TBC = 16
KL = 32


def place_tiles(tiles, cell, usable, cells_all):
    target = jnp.where(usable, cell, -1).astype(jnp.int32)
    select = (target[:, None] == jnp.arange(cells_all, dtype=jnp.int32)[None, :]).astype(
        tiles.dtype
    )
    placed = jnp.einsum("sc,sab->cab", select, tiles, preferred_element_type=jnp.float32)
    return placed.astype(tiles.dtype)


def unpack_list(tiles, place, count):
    tile_side = tiles.shape[-1]
    slot_count = tiles.shape[3]
    flat_tiles = tiles.reshape(-1, tile_side, tile_side)
    flat_place = place.reshape(-1)
    shard_of = jnp.arange(flat_place.shape[0], dtype=jnp.int32) // slot_count
    slot_of = jnp.arange(flat_place.shape[0], dtype=jnp.int32) % slot_count
    usable = slot_of < jnp.repeat(count.reshape(-1), slot_count)
    return (flat_tiles, flat_place, shard_of, usable)


def tile_product(left_grid, right_grid):
    return jnp.einsum("ikab,kjbc->iajc", left_grid, right_grid, preferred_element_type=jnp.float32)


def shards(a_tiles, a_place, a_count, b_tiles, b_place, b_count, out_place):
    tile_side = a_tiles.shape[-1]
    span_a = KL // lax.axis_size("col")
    span_b = KL // lax.axis_size("row")
    b_whole = (
        lax.all_gather(b_tiles, "row", axis=1, tiled=True),
        lax.all_gather(b_place, "row", axis=1, tiled=True),
        lax.all_gather(b_count, "row", axis=1, tiled=True),
    )
    b_flat, b_where, b_shard, b_usable = unpack_list(b_whole[0], b_whole[1], b_whole[2])
    b_cell = (b_shard * span_b + b_where // TBC) * TBC + b_where % TBC
    b_grid = place_tiles(b_flat, b_cell, b_usable, KL * TBC).reshape(KL, TBC, tile_side, tile_side)
    piece = (
        lax.all_gather(a_tiles, "col", axis=2, tiled=True),
        lax.all_gather(a_place, "col", axis=2, tiled=True),
        lax.all_gather(a_count, "col", axis=2, tiled=True),
    )
    width = piece[0].shape[2] * span_a
    a_flat, a_where, a_shard, a_usable = unpack_list(piece[0], piece[1], piece[2])
    a_cell = a_where // span_a * width + a_shard * span_a + a_where % span_a
    a_grid = place_tiles(a_flat, a_cell, a_usable, TB * width).reshape(
        TB, width, tile_side, tile_side
    )
    partial_sum = tile_product(a_grid, b_grid)
    pattern = out_place.reshape(-1)
    half_count = pattern.shape[0] // lax.axis_size("layer")
    summed = lax.psum(partial_sum, "layer")
    owned = lax.dynamic_slice_in_dim(pattern, lax.axis_index("layer") * half_count, half_count)
    result = summed[owned // TBC, :, owned % TBC, :]
    return result.astype(jnp.bfloat16).reshape(1, 1, half_count, tile_side, tile_side)


def solution(mesh):
    return jax.shard_map(
        shards,
        mesh=mesh,
        in_specs=(
            P("row", "layer", "col", None, None, None),
            P("row", "layer", "col", None),
            P("row", "layer", "col"),
            P("layer", "row", "col", None, None, None),
            P("layer", "row", "col", None),
            P("layer", "row", "col"),
            P("row", "col", None),
        ),
        out_specs=P("row", "col", "layer", None, None),
        check_vma=False,
    )
```

profile of v0, /device:TPU:0, one launch (start us, length us, event | category | flops | bytes accessed | tf_op | source)
XLA Modules:
  0.0 216.3 jit_solution(13073156992010758464)
XLA Ops:
  6.5 0.0 all-gather.3.cloned.1.call-start
  6.5 0.7 all-gather.3.cloned.1.call-update
  7.3 0.0 all-gather.5.cloned.1.call-start
  7.3 0.7 all-gather.5.cloned.1.call-update
  8.7 1.2 dynamic-slice.2
  9.9 1.3 dynamic-slice.1
  11.9 0.7 bitcast_dynamic-update-slice_fusion
  12.6 0.7 bitcast_dynamic-update-slice_fusion.1
  13.3 8.9 %all-reduce.1 = s32[4]{0:T(128)S(1)} all-reduce(s32[4]{0:T(128)S(1)} %bitcast_dynamic-update-slice_fusion), channel_id=1, replica_groups=mesh['row'=4,'col'=4,'layer'=2] {'row'}, use_global_device_ids=true, to_apply=%add.1 | all-reduce | flops 4 | bytes 32
  22.1 9.2 %all-reduce = s32[4]{0:T(128)S(1)} all-reduce(s32[4]{0:T(128)S(1)} %bitcast_dynamic-update-slice_fusion.1), channel_id=1, replica_groups=mesh['row'=4,'col'=4,'layer'=2] {'col'}, use_global_device_ids=true, to_apply=%add | all-reduce | flops 4 | bytes 32
  31.3 0.1 broadcast_in_dim.9
  31.4 0.1 reshape.327
  31.4 7.9 %all_gather.22 = s32[1,4,1,64]{3,2,0,1:T(1,128)S(1)} all-gather(s32[1,1,1,64]{3,2,0,1:T(1,128)} %bitcast.60), channel_id=1, replica_groups=mesh['row'=4,'col'=4,'layer'=2] {'row'}, dimensions={1}, use_global_device_ids=true | all-gather | bytes 1280 | tf_op jit(solution)/shard_map/all_gather | solution.py:41
  39.3 0.5 broadcast.372
  39.8 0.7 reduce.6
  40.5 0.1 reshape.328
  40.6 0.1 broadcast_in_dim.8
  40.6 0.1 reshape.322
  40.7 8.9 %all_gather.19 = s32[1,1,4,16]{3,1,0,2:T(1,128)S(1)} all-gather(s32[1,1,1,16]{3,1,0,2:T(1,128)} %bitcast.61), channel_id=1, replica_groups=mesh['row'=4,'col'=4,'layer'=2] {'col'}, dimensions={2}, use_global_device_ids=true | all-gather | bytes 320 | tf_op jit(solution)/shard_map/all_gather | solution.py:49
  49.7 0.7 reduce.7
  50.3 0.1 reshape.323
  50.4 0.7 fusion.27
  51.2 6.5 %all-gather.3.cloned.1.call-done = bf16[1,1,4,16,128,128]{5,4,3,1,0,2:T(8,128)(2,1)} async-done(((bf16[1,1,1,16,128,128]{5,4,3,1,0,2:T(8,128)(2,1)}), bf16[1,1,4,16,128,128]{5,4,3,1,0,2:T(8,128)(2,1)}) %all-gather.3.cloned.1.call-update) | async-done | bytes 2097168 | tf_op jit(solution)/shard_map/all_gather | solution.py:48
  57.7 2.9 %copy.14 = bf16[1,1,4,16,128,128]{5,3,2,4,1,0:T(8,128)(2,1)S(1)} copy(bf16[1,1,4,16,128,128]{5,4,3,1,0,2:T(8,128)(2,1)} %all-gather.3.cloned.1.call-done) | data formatting | bytes 4194304 | tf_op jit(solution)/shard_map/all_gather | solution.py:48
  60.7 3.3 %convolution_convert_fusion.1 = bf16[128,128,128]{2,0,1:T(8,128)(2,1)} fusion(bf16[64,128,128]{2,0,1:T(8,128)(2,1)S(1)} %bitcast.56, s32[64]{0:T(128)S(1)} %compare_select_fusion.3), kind=kOutput, calls=%fused_computation.6 | convolution fusion | flops 270540800 | bytes 6291712 | tf_op jit(solution)/shard_map/sc,sab->cab/dot_general | solution.py:16
  64.0 81.9 %all-gather.5.cloned.1.call-done = bf16[1,4,1,64,128,128]{5,4,3,2,0,1:T(8,128)(2,1)} async-done(((bf16[1,1,1,64,128,128]{5,4,3,2,0,1:T(8,128)(2,1)}), bf16[1,4,1,64,128,128]{5,4,3,2,0,1:T(8,128)(2,1)}) %all-gather.5.cloned.1.call-update) | async-done | bytes 8388624 | tf_op jit(solution)/shard_map/all_gather | solution.py:40
  145.9 12.0 %copy.17 = bf16[1,4,1,64,128,128]{5,3,1,4,2,0:T(8,128)(2,1)} copy(bf16[1,4,1,64,128,128]{5,4,3,2,0,1:T(8,128)(2,1)} %all-gather.5.cloned.1.call-done) | data formatting | bytes 16777216 | tf_op jit(solution)/shard_map/all_gather | solution.py:40
  157.9 11.6 %convolution_convert_fusion = bf16[512,128,128]{2,0,1:T(8,128)(2,1)} fusion(bf16[256,128,128]{2,0,1:T(8,128)(2,1)} %bitcast.54, s32[256]{0:T(256)S(1)} %compare_select_fusion.2), kind=kOutput, calls=%fused_computation.4 | convolution fusion | flops 4303486976 | bytes 25166848 | tf_op jit(solution)/shard_map/sc,sab->cab/dot_general | solution.py:16
  169.5 0.0 copy-done
  169.5 23.6 %fusion.4 = f32[4,128,16,128]{3,1,2,0:T(8,128)} fusion(bf16[32,16,128,128]{3,1,0,2:T(8,128)(2,1)} %bitcast.55, bf16[4,32,128,128,1]{3,1,0,2,4:T(8,128)(2,1)S(1)} %bitcast.57), kind=kOutput, calls=%fused_computation.7 | convolution fusion | flops 8589934592 | bytes 25165824 | tf_op jit(solution)/shard_map/ikab,kjbc->iajc/dot_general | solution.py:32
  193.2 14.9 %all-reduce.3 = bf16[4,128,16,128]{3,1,2,0:T(8,128)(2,1)S(1)} all-reduce(f32[4,128,16,128]{3,1,2,0:T(8,128)} %fusion.4), channel_id=1, replica_groups=mesh['row'=4,'col'=4,'layer'=2] {'layer'}, use_global_device_ids=true, to_apply=%region_0.1 | all-reduce | flops 1048576 | bytes 6291456 | tf_op jit(solution)/shard_map/psum | solution.py:61
  208.1 1.4 gather_fusion
  (5 shorter events, 0.0 us)
Async XLA Ops:
  6.5 51.2 %all-gather.3.cloned.1.call-start = ((), (), s32[]{:S(2)}) async-start(), calls=%async_computation | async-start | bytes 2621440 | tf_op jit(solution)/shard_map/all_gather | solution.py:48
  7.3 138.7 %all-gather.5.cloned.1.call-start = ((), (), s32[]{:S(2)}) async-start(), calls=%async_computation.1 | async-start | bytes 10485760 | tf_op jit(solution)/shard_map/all_gather | solution.py:40
  157.9 11.6 %copy-start = (bf16[128,128,128]{2,0,1:T(8,128)(2,1)S(1)}, bf16[128,128,128]{2,0,1:T(8,128)(2,1)}, u32[]{:S(2)}) copy-start(bf16[128,128,128]{2,0,1:T(8,128)(2,1)} %convolution_convert_fusion.1) | copy-start | bytes 12582916
Sparse Core Ops, SparseCore 0:
  8.9 48.7 all-gather.2
  59.6 86.3 all-gather.4
where the time goes:
time: 217 us; the launch traced here: 216 us
  waiting for transfers between devices  89.9 us (41%)
  blocking collectives  49.7 us (23%)
  matrix products  38.5 us (18%)
  local copies, waits for them, and re-layouts  21.3 us (10%)
  between operations  14.8 us (7%)
    all_gather x1, waiting for transfers between devices, shards(): lax.all_gather(b_tiles, 'row', axis=1, tiled=True)  81.9 us
    dot_general x1, matrix products, tile_product(): jnp.einsum('ikab,kjbc->iajc', left_grid, right_grid, preferred_element_ty...  23.6 us
    unnamed x2, blocking collectives  18 us
    dot_general x2, matrix products, place_tiles(): jnp.einsum('sc,sab->cab', select, tiles, preferred_element_type=jnp.float32)  14.9 us
    psum x1, blocking collectives, shards(): summed = lax.psum(partial_sum, 'layer')  14.9 us
    all_gather x1, local copies, waits for them, and re-layouts, shards(): lax.all_gather(b_tiles, 'row', axis=1, tiled=True)  12 us
    all_gather x1, blocking collectives, shards(): lax.all_gather(a_place, 'col', axis=2, tiled=True)  8.95 us
    all_gather x1, blocking collectives, shards(): lax.all_gather(b_place, 'row', axis=1, tiled=True)  7.86 us
  transfers between devices with their start and end apart: 2, of which 2 were waited for; matrix products, arithmetic and copies ran while one was open for 6% of the time, Pallas kernels for 0%

commit v1 on v0

--- a/solution.py
+++ b/solution.py
@@ -1,11 +1,14 @@
 import jax
 import jax.numpy as jnp
 from jax import lax
+from jax.experimental import pallas as pl
+from jax.experimental.pallas import tpu as pltpu
 from jax.sharding import PartitionSpec as P
 
 TB = 4
 TBC = 16
 KL = 32
+WIDE = 4
 
 
 def place_tiles(tiles, cell, usable, cells_all):
@@ -32,7 +35,7 @@
     return jnp.einsum("ikab,kjbc->iajc", left_grid, right_grid, preferred_element_type=jnp.float32)
 
 
-def shards(a_tiles, a_place, a_count, b_tiles, b_place, b_count, out_place):
+def gathered_shards(a_tiles, a_place, a_count, b_tiles, b_place, b_count, out_place):
     tile_side = a_tiles.shape[-1]
     span_a = KL // lax.axis_size("col")
     span_b = KL // lax.axis_size("row")
@@ -64,9 +67,220 @@
     return result.astype(jnp.bfloat16).reshape(1, 1, half_count, tile_side, tile_side)
 
 
+def across(x, axes, pairs):
+    return lax.ppermute(x, axes, pairs)
+
+
+def flip(x, bits):
+    return across(x, "row", [(i, i ^ bits) for i in range(4)])
+
+
+def swap_layers(x):
+    return across(x, "layer", [(0, 1), (1, 0)])
+
+
+def slot_table(place, count, cells):
+    slots = place.shape[-1]
+    slot = jnp.arange(slots, dtype=jnp.int32)
+    hit = (place[:, :, None] == jnp.arange(cells, dtype=jnp.int32)) & (
+        slot[None, :, None] < count[:, None, None]
+    )
+    return slots - jnp.sum(jnp.where(hit, slots - slot[None, :, None], 0), axis=1)
+
+
+def rows_of(left, table, entry, tiles, span):
+    height, side = tiles.shape[-2:]
+    for i in range(TB):
+        for k in range(span):
+            left[i * height : (i + 1) * height, k * side : (k + 1) * side] = tiles[
+                table[entry, i * span + k]
+            ]
+
+
+def block_of(left, table, entry, tiles, span, first):
+    right = jnp.concatenate(
+        [
+            jnp.concatenate([tiles[table[entry, k * TBC + first + j]] for j in range(WIDE)], axis=1)
+            for k in range(span)
+        ],
+        axis=0,
+    )
+    return jnp.dot(left[...], right, preferred_element_type=jnp.float32)
+
+
+def put_block(grid, first, value):
+    side = grid.shape[-1]
+    for j in range(WIDE):
+        grid[first + j] = value[:, j * side : (j + 1) * side]
+
+
+def pick(out, grid, table, entry, first):
+    height = out.shape[-2]
+
+    def one(o, carry):
+        place = table[entry, first + o]
+        out[o] = grid[place % TBC, pl.ds(pl.multiple_of((place // TBC) * height, height), height), :]
+        return carry
+
+    lax.fori_loop(0, out.shape[0], one, 0, unroll=True)
+
+
+def note_tile(dtype, height, side, *numbers):
+    note = jnp.concatenate([n.reshape(-1) for n in numbers])
+    note = jnp.pad(note, (0, side - note.size)).astype(dtype)
+    return jnp.broadcast_to(note, (1, height, side))
+
+
+def note_of(tiles, at):
+    return tiles[at, 0].astype(jnp.int32)
+
+
+def planned_shards(a_tiles, a_place, a_count, b_tiles, b_place, b_count, out_place):
+    side = a_tiles.shape[-1]
+    na, nb, no = a_place.shape[-1], b_place.shape[-1], out_place.shape[-1]
+    row, col, layer = (lax.axis_index(n).astype(jnp.int32) for n in ("row", "col", "layer"))
+    span, half, low = KL // 4, no // 2, side // 2
+    inner = span * side
+
+    b = b_tiles.reshape(nb, side, side)
+    b_x, b_y = flip(b, 1), flip(b, 2)
+    a = a_tiles.reshape(na, side, side)
+    a = jnp.concatenate(
+        [a, jnp.zeros((1, side, side), a.dtype), note_tile(a.dtype, side, side, a_place, a_count)]
+    )
+    two = across(a, "col", [(c, c ^ 2) for c in range(4)])
+    one, three = (across(g, "col", [(c, c ^ 1) for c in range(4)]) for g in (a, two))
+    a_got, b_x, b_y = lax.optimization_barrier(([a, one, two, three], b_x, b_y))
+    spare = lax.select_n(col ^ row ^ 3, *a_got)
+    b_note = note_tile(b.dtype, low, side, b_place, b_count, out_place)
+    upper, lower = (jnp.concatenate([g, b_note]) for g in (spare[:, :low], spare[:, low:]))
+    upper, lower = flip(upper, 1), flip(lower, 2)
+    upper, lower, b_x, b_y, a_got = lax.optimization_barrier((upper, lower, b_x, b_y, a_got))
+
+    a_notes = jnp.stack([note_of(g, na + 1) for g in a_got])
+    lefts = jnp.stack(
+        [lax.dynamic_index_in_dim(a_notes, col ^ row ^ q, keepdims=False) for q in range(3)]
+        + [note_of(upper, na + 1), note_of(lower, na + 1)]
+    )
+    left_table = slot_table(lefts[:, :na], lefts[:, na], TB * span)
+    rights = jnp.stack([note_of(g, -1) for g in (b_note, upper, lower)])
+    right_table = slot_table(rights[:, :nb], rights[:, nb], span * TBC)
+    places = rights[:, nb + 1 : nb + 1 + no]
+    table = jnp.concatenate(
+        [
+            jnp.pad(left_table, ((0, 0), (0, side - TB * span))),
+            right_table,
+            jnp.pad(places, ((0, 0), (0, side - no))),
+            jnp.pad(jnp.stack([row, col, layer]), (0, side - 3))[None],
+        ]
+    )
+
+    at_right, at_place, at_where = 5, 8, 11
+
+    def load_rights(refs, tiles, sems):
+        copies = [
+            pltpu.make_async_copy(ref, tiles.at[n, 0:nb], sems.at[n]) for n, ref in enumerate(refs)
+        ]
+        for n, c in enumerate(copies):
+            c.start()
+            tiles[n, nb] = jnp.zeros((side, side), tiles.dtype)
+        return copies
+
+    def help_neighbours(table, upper, lower, b_y, b_x, keep, give, left, total, tiles, sems):
+        copies = load_rights((b_y, b_x), tiles, sems)
+        layer = table[at_where, 2]
+        for q, shard in enumerate((upper, lower)):
+            rows_of(left.at[q], table, 3 + q, shard, span)
+        for q in range(2):
+            copies[q].wait()
+            for first in range(0, TBC, WIDE):
+                part = block_of(left.at[q], table, at_right + 2 - q, tiles.at[q], span, first)
+                put_block(total.at[q], first, part)
+        for q in range(2):
+            pick(give.at[q], total.at[q], table, at_place + 1 + q, (1 - layer) * half)
+            pick(keep.at[q], total.at[q], table, at_place + 1 + q, layer * half)
+
+    def own_rows(table, *refs):
+        lefts, rights = refs[0:4], refs[4:7]
+        keep, give, left, total, tiles, sems = refs[7:]
+        copies = load_rights(rights, tiles, sems)
+        row, col, layer = (table[at_where, n] for n in range(3))
+        for e in range(4):
+            q = e ^ col ^ row
+
+            @pl.when(q < 3)
+            def _():
+                rows_of(left.at[q], table, q, lefts[e], span)
+
+        for c in copies:
+            c.wait()
+        for first in range(0, TBC, WIDE):
+            acc = block_of(left.at[0], table, at_right, tiles.at[0], span, first)
+            for q in (1, 2):
+                acc = acc + block_of(left.at[q], table, at_right + q, tiles.at[q], span, first)
+            put_block(total, first, acc)
+        pick(give, total, table, at_place, (1 - layer) * half)
+        pick(keep, total, table, at_place, layer * half)
+
+    smem = pl.BlockSpec(memory_space=pltpu.SMEM)
+    vmem = pl.BlockSpec(memory_space=pltpu.VMEM)
+    hbm = pl.BlockSpec(memory_space=pltpu.HBM)
+
+    def call(kernel, lefts, rights, out, left_blocks, height, grids):
+        return pl.pallas_call(
+            kernel,
+            in_specs=[smem] + [vmem] * len(lefts) + [hbm] * len(rights),
+            out_specs=(vmem, vmem),
+            out_shape=(out, out),
+            scratch_shapes=[
+                pltpu.VMEM((left_blocks, TB * height, inner), a.dtype),
+                pltpu.VMEM(grids + (TBC, TB * height, side), jnp.float32),
+                pltpu.VMEM((len(rights), nb + 1, side, side), b.dtype),
+                pltpu.SemaphoreType.DMA((len(rights),)),
+            ],
+            compiler_params=pltpu.CompilerParams(vmem_limit_bytes=24 * 2**20),
+            cost_estimate=pl.CostEstimate(
+                flops=2 * left_blocks * TB * height * inner * TBC * side,
+                bytes_accessed=sum(g.size for g in (*lefts, *rights)) * 2,
+                transcendentals=0,
+            ),
+            name=kernel.__name__,
+        )(table, *lefts, *rights)
+
+    part_keep, part_give = call(
+        help_neighbours,
+        (upper, lower),
+        (b_y, b_x),
+        jax.ShapeDtypeStruct((2, half, low, side), jnp.float32),
+        2,
+        low,
+        (2,),
+    )
+    part_sum = part_keep + swap_layers(part_give)
+    part_sum, b_x, b_y, a_got = lax.optimization_barrier((part_sum, b_x, b_y, a_got))
+    from_x, from_y = flip(part_sum[0], 1), flip(part_sum[1], 2)
+    keep, give = call(
+        own_rows,
+        a_got,
+        (b, b_x, b_y),
+        jax.ShapeDtypeStruct((half, side, side), jnp.float32),
+        3,
+        side,
+        (),
+    )
+    give, from_x, from_y = lax.optimization_barrier((give, from_x, from_y))
+    mine = keep + swap_layers(give)
+    result = jnp.concatenate([mine[:, :low] + from_x, mine[:, low:] + from_y], axis=1)
+    return result.astype(jnp.bfloat16).reshape(1, 1, half, side, side)
+
+
 def solution(mesh):
+    if mesh.shape["row"] == 4 and mesh.shape["col"] == 4:
+        body = planned_shards
+    else:
+        body = gathered_shards
     return jax.shard_map(
-        shards,
+        body,
         mesh=mesh,
         in_specs=(
             P("row", "layer", "col", None, None, None),

time: 217 us -> 87 us (0.40)
  blocking collectives: 49.7 us -> 0 us
  waiting for transfers between devices: 89.9 us -> 50.1 us
  matrix products: 38.5 us -> 0 us
  local copies, waits for them, and re-layouts: 21.3 us -> 0.74 us
  Pallas kernels: 0 us -> 14.8 us
  starting transfers between devices: 0.04 us -> 14.4 us
  between operations: 14.8 us -> 1.49 us
  other arithmetic: 2.1 us -> 5.36 us
    all_gather x2 -> x0, waiting for transfers between devices: 88.5 us -> none  [the longest x1 81.9 us: shards(): lax.all_gather(b_tiles, 'row', axis=1, tiled=True)]
    ppermute x0 -> x11, waiting for transfers between devices: none -> 50.1 us  [across(): return lax.ppermute(x, axes, pairs)]
    dot_general x3 -> x0, matrix products: 38.5 us -> none  [the longest x1 23.6 us: tile_product(): jnp.einsum('ikab,kjbc->iajc', left_grid, right_grid, preferred_element_ty...]
    unnamed x2 -> x0, blocking collectives: 18 us -> none
    all_gather x2 -> x0, blocking collectives: 16.8 us -> none  [the longest x1 8.95 us: shards(): lax.all_gather(a_place, 'col', axis=2, tiled=True)]
    all_gather x3 -> x0, local copies, waits for them, and re-layouts: 15.5 us -> none  [the longest x1 12 us: shards(): lax.all_gather(b_tiles, 'row', axis=1, tiled=True)]
    psum x1 -> x0, blocking collectives: 14.9 us -> none  [shards(): summed = lax.psum(partial_sum, 'layer')]
    pallas_call x0 -> x2, Pallas kernels: none -> 14.8 us  [call(): pl.pallas_call(kernel, in_specs=[smem] + [vmem] * len(lefts) + [hbm] * le...]
  transfers between devices with their start and end apart: 2 -> 11, of which waited for: 2 -> 9; matrix products, arithmetic and copies ran while one was open for 6% -> 4% of each run, Pallas kernels for 0% -> 11%
where the time goes in v1:
time: 87 us; the launch traced here: 86.8 us
  waiting for transfers between devices  50.1 us (58%)
  Pallas kernels  14.8 us (17%)
  starting transfers between devices  14.4 us (17%)
  other arithmetic  5.36 us (6%)
  between operations  1.49 us (2%)
    ppermute x11, waiting for transfers between devices, across(): return lax.ppermute(x, axes, pairs)  50.1 us
    pallas_call x2, Pallas kernels, call(): pl.pallas_call(kernel, in_specs=[smem] + [vmem] * len(lefts) + [hbm] * le...  14.8 us
    ppermute x11, starting transfers between devices, across(): return lax.ppermute(x, axes, pairs)  14.4 us
    reshape x3, other arithmetic, note_tile(): note = jnp.concatenate([n.reshape(-1) for n in numbers])  1.98 us
  transfers between devices with their start and end apart: 11, of which 9 were waited for; matrix products, arithmetic and copies ran while one was open for 4% of the time, Pallas kernels for 11%

profile of v1, /device:TPU:0, one launch (start us, length us, event | category | flops | bytes accessed | tf_op | source)
XLA Modules:
  0.0 86.8 jit_solution(13380569677354525675)
XLA Ops:
  0.0 3.0 %collective-permute-start.4 = (bf16[64,128,128]{2,1,0:T(8,128)(2,1)}, bf16[64,128,128]{2,1,0:T(8,128)(2,1)}, u32[]{:S(2)}, u32[]{:S(2)}) collective-permute-start(bf16[64,128,128]{2,1,0:T(8,128)(2,1)} %bitcast.46), channel_id=1, source_target_pairs={{0,16},{8,24},{16,0},{24,8},{1,17},{9,25},{17,1},{25,9},{2,18},{10... | collective-permute-start | bytes 6291464 | tf_op jit(solution)/shard_map/ppermute | solution.py:71
  3.0 1.5 %collective-permute-start.3 = (bf16[64,128,128]{2,1,0:T(8,128)(2,1)}, bf16[64,128,128]{2,1,0:T(8,128)(2,1)}, u32[]{:S(2)}, u32[]{:S(2)}) collective-permute-start(bf16[64,128,128]{2,1,0:T(8,128)(2,1)} %bitcast.47), channel_id=1, source_target_pairs={{0,8},{8,0},{16,24},{24,16},{1,9},{9,1},{17,25},{25,17},{2,10},{10... | collective-permute-start | bytes 6291464 | tf_op jit(solution)/shard_map/ppermute | solution.py:71
  5.2 0.7 convert_bitcast_fusion.2
  5.9 1.2 %pad_maximum_fusion.refs_0_ = bf16[18,128,128]{2,1,0:T(8,128)(2,1)S(1)} fusion(bf16[1,128,128]{2,1,0:T(8,128)(2,1)S(1)} %broadcast_in_dim.45, bf16[16,128,128]{2,1,0:T(8,128)(2,1)} %bitcast.49, bf16[18]{0:T(256)(128)(2,1)S(1)} %pad.51.clone), kind=kLoop, calls=%fused_computation | loop fusion | flops 589824 | bytes 1146916 | tf_op jit(solution)/shard_map/concatenate | solution.py:148
  7.1 2.7 %collective-permute-start.1 = (bf16[18,128,128]{2,1,0:T(8,128)(2,1)S(1)}, bf16[18,128,128]{2,1,0:T(8,128)(2,1)S(1)}, u32[]{:S(2)}, u32[]{:S(2)}) collective-permute-start(bf16[18,128,128]{2,1,0:T(8,128)(2,1)S(1)} %pad_maximum_fusion.refs_0_), channel_id=1, source_target_pairs={{0,4},{2,6},{4,0},{6,2},{1,5},{3,7},{5,1},{7,3},{8,12},{10,14},{12... | collective-permute-start | bytes 1769480 | tf_op jit(solution)/shard_map/ppermute | solution.py:71
  9.8 1.6 %collective-permute-start = (bf16[18,128,128]{2,1,0:T(8,128)(2,1)S(1)}, bf16[18,128,128]{2,1,0:T(8,128)(2,1)S(1)}, u32[]{:S(2)}, u32[]{:S(2)}) collective-permute-start(bf16[18,128,128]{2,1,0:T(8,128)(2,1)S(1)} %pad_maximum_fusion.refs_0_), channel_id=1, source_target_pairs={{0,2},{2,0},{4,6},{6,4},{1,3},{3,1},{5,7},{7,5},{8,10},{10,8},{12,... | collective-permute-start | bytes 1769480 | tf_op jit(solution)/shard_map/ppermute | solution.py:71
  11.3 24.0 %collective-permute-done.1.refs_2_ = bf16[18,128,128]{2,1,0:T(8,128)(2,1)S(1)} collective-permute-done((bf16[18,128,128]{2,1,0:T(8,128)(2,1)S(1)}, bf16[18,128,128]{2,1,0:T(8,128)(2,1)S(1)}, u32[]{:S(2)}, u32[]{:S(2)}) %collective-permute-start.1) | collective-permute-done | bytes 589856 | tf_op jit(solution)/shard_map/ppermute | solution.py:71
  35.3 0.6 collective-permute-start.2
  35.9 0.7 convert_bitcast_fusion.1
  37.2 0.7 convert_bitcast_fusion
  38.0 11.4 %collective-permute-done.2.refs_3_ = bf16[18,128,128]{2,1,0:T(8,128)(2,1)S(1)} collective-permute-done((bf16[18,128,128]{2,1,0:T(8,128)(2,1)S(1)}, bf16[18,128,128]{2,1,0:T(8,128)(2,1)S(1)}, u32[]{:S(2)}, u32[]{:S(2)}) %collective-permute-start.2) | collective-permute-done | bytes 589856 | tf_op jit(solution)/shard_map/ppermute | solution.py:71
  49.4 0.9 %collective-permute-done.3.b_x.refs_5_ = bf16[64,128,128]{2,1,0:T(8,128)(2,1)} collective-permute-done((bf16[64,128,128]{2,1,0:T(8,128)(2,1)}, bf16[64,128,128]{2,1,0:T(8,128)(2,1)}, u32[]{:S(2)}, u32[]{:S(2)}) %collective-permute-start.3) | collective-permute-done | bytes 2097184 | tf_op jit(solution)/shard_map/ppermute | solution.py:71
  50.4 0.1 select_select_fusion
  50.6 0.4 collective-permute-start.6
  51.0 1.7 %collective-permute-start.5 = (bf16[19,64,128]{2,1,0:T(8,128)(2,1)S(1)}, bf16[19,64,128]{2,1,0:T(8,128)(2,1)S(1)}, u32[]{:S(2)}, u32[]{:S(2)}) collective-permute-start(bf16[19,64,128]{2,1,0:T(8,128)(2,1)S(1)} %get-tuple-element.72), channel_id=1, source_target_pairs={{0,8},{8,0},{16,24},{24,16},{1,9},{9,1},{17,25},{25,17},{2,10},{10... | collective-permute-start | bytes 933896 | tf_op jit(solution)/shard_map/ppermute | solution.py:71
  52.8 5.8 %collective-permute-done.6.lower = bf16[19,64,128]{2,1,0:T(8,128)(2,1)S(1)} collective-permute-done((bf16[19,64,128]{2,1,0:T(8,128)(2,1)S(1)}, bf16[19,64,128]{2,1,0:T(8,128)(2,1)S(1)}, u32[]{:S(2)}, u32[]{:S(2)}) %collective-permute-start.6) | collective-permute-done | bytes 311328 | tf_op jit(solution)/shard_map/ppermute | solution.py:71
  58.6 0.3 collective-permute-done.5.upper
  58.9 0.2 slice_reduce_fusion.1
  59.3 0.1 select_reduce_fusion
  59.5 0.2 slice_reduce_fusion
  59.9 4.9 %help_neighbours.1 = (f32[2,16,64,128]{3,2,1,0:T(8,128)S(1)}, f32[2,16,64,128]{3,2,1,0:T(8,128)S(1)}) custom-call(s32[12,128]{1,0:T(8,128)S(1)} %fusion.6.table, bf16[19,64,128]{2,1,0:T(8,128)(2,1)S(1)} %collective-permute-done.5.upper, bf16[19,64,128]{2,1,0:T(8,128)(2,1)S(1)} %collective-permute-done.6.lower, ...), custom_call_target="tpu_custom_call" | custom-call | flops 2147483648 | bytes 4816896 | tf_op jit(solution)/shard_map/help_neighbours/pallas_call | solution.py:230
  64.9 2.6 %collective-permute-done.7 = f32[2,16,64,128]{3,2,1,0:T(8,128)S(1)} collective-permute-done((f32[2,16,64,128]{3,2,1,0:T(8,128)S(1)}, f32[2,16,64,128]{3,2,1,0:T(8,128)S(1)}, u32[]{:S(2)}, u32[]{:S(2)}) %collective-permute-start.7) | collective-permute-done | bytes 1048608 | tf_op jit(solution)/shard_map/ppermute | solution.py:71
  67.6 0.2 add.35
  67.9 1.5 %collective-permute-start.9 = (f32[16,64,128]{2,1,0:T(8,128)S(1)}, f32[16,64,128]{2,1,0:T(8,128)S(1)}, u32[]{:S(2)}, u32[]{:S(2)}) collective-permute-start(f32[16,64,128]{2,1,0:T(8,128)S(1)} %get-tuple-element.63), channel_id=1, source_target_pairs={{0,16},{8,24},{16,0},{24,8},{1,17},{9,25},{17,1},{25,9},{2,18},{10... | collective-permute-start | bytes 1572872 | tf_op jit(solution)/shard_map/ppermute | solution.py:71
  69.4 1.5 %collective-permute-start.8 = (f32[16,64,128]{2,1,0:T(8,128)S(1)}, f32[16,64,128]{2,1,0:T(8,128)S(1)}, u32[]{:S(2)}, u32[]{:S(2)}) collective-permute-start(f32[16,64,128]{2,1,0:T(8,128)S(1)} %get-tuple-element.64), channel_id=1, source_target_pairs={{0,8},{8,0},{16,24},{24,16},{1,9},{9,1},{17,25},{25,17},{2,10},{10... | collective-permute-start | bytes 1572872 | tf_op jit(solution)/shard_map/ppermute | solution.py:71
  70.8 9.9 %own_rows.1 = (f32[16,128,128]{2,1,0:T(8,128)S(1)}, f32[16,128,128]{2,1,0:T(8,128)S(1)}) custom-call(s32[12,128]{1,0:T(8,128)S(1)} %fusion.6.table, bf16[18,128,128]{2,1,0:T(8,128)(2,1)S(1)} %pad_maximum_fusion.refs_0_, bf16[18,128,128]{2,1,0:T(8,128)(2,1)S(1)} %collective-permute-done.refs_1_, bf16[18,128,128]{2,1,0:T(8,128)(2,1)S(1)} %collective-permute-done.1.refs_2_, ...), custom_call_target="tpu_custom_call" | custom-call | flops 6442450944 | bytes 8650752 | tf_op jit(solution)/shard_map/own_rows/pallas_call | solution.py:230
  80.7 1.2 %collective-permute-done.9 = f32[16,64,128]{2,1,0:T(8,128)S(1)} collective-permute-done((f32[16,64,128]{2,1,0:T(8,128)S(1)}, f32[16,64,128]{2,1,0:T(8,128)S(1)}, u32[]{:S(2)}, u32[]{:S(2)}) %collective-permute-start.9) | collective-permute-done | bytes 524320 | tf_op jit(solution)/shard_map/ppermute | solution.py:71
  81.9 1.1 %collective-permute-done.8 = f32[16,64,128]{2,1,0:T(8,128)S(1)} collective-permute-done((f32[16,64,128]{2,1,0:T(8,128)S(1)}, f32[16,64,128]{2,1,0:T(8,128)S(1)}, u32[]{:S(2)}, u32[]{:S(2)}) %collective-permute-start.8) | collective-permute-done | bytes 524320 | tf_op jit(solution)/shard_map/ppermute | solution.py:71
  83.0 2.7 %collective-permute-done.10 = f32[16,128,128]{2,1,0:T(8,128)S(1)} collective-permute-done((f32[16,128,128]{2,1,0:T(8,128)S(1)}, f32[16,128,128]{2,1,0:T(8,128)S(1)}, u32[]{:S(2)}, u32[]{:S(2)}) %collective-permute-start.10) | collective-permute-done | bytes 1048608 | tf_op jit(solution)/shard_map/ppermute | solution.py:71
  85.7 0.1 add.36
  85.8 0.2 fusion.2
  86.0 0.8 pad_maximum_fusion.1
  (33 shorter events, 1.1 us)
Async XLA Ops:
  0.0 49.4 %collective-permute-start.4 = (bf16[64,128,128]{2,1,0:T(8,128)(2,1)}, bf16[64,128,128]{2,1,0:T(8,128)(2,1)}, u32[]{:S(2)}, u32[]{:S(2)}) collective-permute-start(bf16[64,128,128]{2,1,0:T(8,128)(2,1)} %bitcast.46), channel_id=1, source_target_pairs={{0,16},{8,24},{16,0},{24,8},{1,17},{9,25},{17,1},{25,9},{2,18},{10... | collective-permute-start | bytes 6291464 | tf_op jit(solution)/shard_map/ppermute | solution.py:71
  3.0 47.4 %collective-permute-start.3 = (bf16[64,128,128]{2,1,0:T(8,128)(2,1)}, bf16[64,128,128]{2,1,0:T(8,128)(2,1)}, u32[]{:S(2)}, u32[]{:S(2)}) collective-permute-start(bf16[64,128,128]{2,1,0:T(8,128)(2,1)} %bitcast.47), channel_id=1, source_target_pairs={{0,8},{8,0},{16,24},{24,16},{1,9},{9,1},{17,25},{25,17},{2,10},{10... | collective-permute-start | bytes 6291464 | tf_op jit(solution)/shard_map/ppermute | solution.py:71
  7.1 28.2 %collective-permute-start.1 = (bf16[18,128,128]{2,1,0:T(8,128)(2,1)S(1)}, bf16[18,128,128]{2,1,0:T(8,128)(2,1)S(1)}, u32[]{:S(2)}, u32[]{:S(2)}) collective-permute-start(bf16[18,128,128]{2,1,0:T(8,128)(2,1)S(1)} %pad_maximum_fusion.refs_0_), channel_id=1, source_target_pairs={{0,4},{2,6},{4,0},{6,2},{1,5},{3,7},{5,1},{7,3},{8,12},{10,14},{12... | collective-permute-start | bytes 1769480 | tf_op jit(solution)/shard_map/ppermute | solution.py:71
  9.8 28.3 %collective-permute-start = (bf16[18,128,128]{2,1,0:T(8,128)(2,1)S(1)}, bf16[18,128,128]{2,1,0:T(8,128)(2,1)S(1)}, u32[]{:S(2)}, u32[]{:S(2)}) collective-permute-start(bf16[18,128,128]{2,1,0:T(8,128)(2,1)S(1)} %pad_maximum_fusion.refs_0_), channel_id=1, source_target_pairs={{0,2},{2,0},{4,6},{6,4},{1,3},{3,1},{5,7},{7,5},{8,10},{10,8},{12,... | collective-permute-start | bytes 1769480 | tf_op jit(solution)/shard_map/ppermute | solution.py:71
  35.3 14.1 %collective-permute-start.2 = (bf16[18,128,128]{2,1,0:T(8,128)(2,1)S(1)}, bf16[18,128,128]{2,1,0:T(8,128)(2,1)S(1)}, u32[]{:S(2)}, u32[]{:S(2)}) collective-permute-start(bf16[18,128,128]{2,1,0:T(8,128)(2,1)S(1)} %collective-permute-done.1.refs_2_), channel_id=1, source_target_pairs={{0,2},{2,0},{4,6},{6,4},{1,3},{3,1},{5,7},{7,5},{8,10},{10,8},{12,... | collective-permute-start | bytes 1769480 | tf_op jit(solution)/shard_map/ppermute | solution.py:71
  50.6 8.0 %collective-permute-start.6 = (bf16[19,64,128]{2,1,0:T(8,128)(2,1)S(1)}, bf16[19,64,128]{2,1,0:T(8,128)(2,1)S(1)}, u32[]{:S(2)}, u32[]{:S(2)}) collective-permute-start(bf16[19,64,128]{2,1,0:T(8,128)(2,1)S(1)} %get-tuple-element.71), channel_id=1, source_target_pairs={{0,16},{8,24},{16,0},{24,8},{1,17},{9,25},{17,1},{25,9},{2,18},{10... | collective-permute-start | bytes 933896 | tf_op jit(solution)/shard_map/ppermute | solution.py:71
  51.0 7.9 %collective-permute-start.5 = (bf16[19,64,128]{2,1,0:T(8,128)(2,1)S(1)}, bf16[19,64,128]{2,1,0:T(8,128)(2,1)S(1)}, u32[]{:S(2)}, u32[]{:S(2)}) collective-permute-start(bf16[19,64,128]{2,1,0:T(8,128)(2,1)S(1)} %get-tuple-element.72), channel_id=1, source_target_pairs={{0,8},{8,0},{16,24},{24,16},{1,9},{9,1},{17,25},{25,17},{2,10},{10... | collective-permute-start | bytes 933896 | tf_op jit(solution)/shard_map/ppermute | solution.py:71
  64.8 2.7 %collective-permute-start.7 = (f32[2,16,64,128]{3,2,1,0:T(8,128)S(1)}, f32[2,16,64,128]{3,2,1,0:T(8,128)S(1)}, u32[]{:S(2)}, u32[]{:S(2)}) collective-permute-start(f32[2,16,64,128]{3,2,1,0:T(8,128)S(1)} %get-tuple-element.48), channel_id=1, source_target_pairs={{0,1},{1,0},{2,3},{3,2},{4,5},{5,4},{6,7},{7,6},{8,9},{9,8},{10,11... | collective-permute-start | bytes 3145736 | tf_op jit(solution)/shard_map/ppermute | solution.py:71
  67.6 3.3 %copy-start = (bf16[1,1,1,64,128,128]{5,4,3,2,1,0:T(8,128)(2,1)S(1)}, bf16[1,1,1,64,128,128]{5,4,3,2,1,0:T(8,128)(2,1)}, u32[]{:S(2)}) copy-start(bf16[1,1,1,64,128,128]{5,4,3,2,1,0:T(8,128)(2,1)} %param.10) | copy-start | bytes 6291460
  67.9 14.0 %collective-permute-start.9 = (f32[16,64,128]{2,1,0:T(8,128)S(1)}, f32[16,64,128]{2,1,0:T(8,128)S(1)}, u32[]{:S(2)}, u32[]{:S(2)}) collective-permute-start(f32[16,64,128]{2,1,0:T(8,128)S(1)} %get-tuple-element.63), channel_id=1, source_target_pairs={{0,16},{8,24},{16,0},{24,8},{1,17},{9,25},{17,1},{25,9},{2,18},{10... | collective-permute-start | bytes 1572872 | tf_op jit(solution)/shard_map/ppermute | solution.py:71
  69.4 13.7 %collective-permute-start.8 = (f32[16,64,128]{2,1,0:T(8,128)S(1)}, f32[16,64,128]{2,1,0:T(8,128)S(1)}, u32[]{:S(2)}, u32[]{:S(2)}) collective-permute-start(f32[16,64,128]{2,1,0:T(8,128)S(1)} %get-tuple-element.64), channel_id=1, source_target_pairs={{0,8},{8,0},{16,24},{24,16},{1,9},{9,1},{17,25},{25,17},{2,10},{10... | collective-permute-start | bytes 1572872 | tf_op jit(solution)/shard_map/ppermute | solution.py:71
  83.0 2.7 %collective-permute-start.10 = (f32[16,128,128]{2,1,0:T(8,128)S(1)}, f32[16,128,128]{2,1,0:T(8,128)S(1)}, u32[]{:S(2)}, u32[]{:S(2)}) collective-permute-start(f32[16,128,128]{2,1,0:T(8,128)S(1)} %get-tuple-element.58), channel_id=1, source_target_pairs={{0,1},{1,0},{2,3},{3,2},{4,5},{5,4},{6,7},{7,6},{8,9},{9,8},{10,11... | collective-permute-start | bytes 3145736 | tf_op jit(solution)/shard_map/ppermute | solution.py:71

commit v2 on v0

--- a/solution.py
+++ b/solution.py
@@ -1,11 +1,14 @@
 import jax
 import jax.numpy as jnp
 from jax import lax
+from jax.experimental import pallas as pl
+from jax.experimental.pallas import tpu as pltpu
 from jax.sharding import PartitionSpec as P
 
 TB = 4
 TBC = 16
 KL = 32
+WIDE = 4
 
 
 def place_tiles(tiles, cell, usable, cells_all):
@@ -32,7 +35,7 @@
     return jnp.einsum("ikab,kjbc->iajc", left_grid, right_grid, preferred_element_type=jnp.float32)
 
 
-def shards(a_tiles, a_place, a_count, b_tiles, b_place, b_count, out_place):
+def gathered_shards(a_tiles, a_place, a_count, b_tiles, b_place, b_count, out_place):
     tile_side = a_tiles.shape[-1]
     span_a = KL // lax.axis_size("col")
     span_b = KL // lax.axis_size("row")
@@ -64,9 +67,294 @@
     return result.astype(jnp.bfloat16).reshape(1, 1, half_count, tile_side, tile_side)
 
 
+def across(x, axes, pairs):
+    return lax.ppermute(x, axes, pairs)
+
+
+def flip(x, bits):
+    return across(x, "row", [(i, i ^ bits) for i in range(4)])
+
+
+def swap_layers(x):
+    return across(x, "layer", [(0, 1), (1, 0)])
+
+
+def rows_of(left, table, entry, shard, height):
+    side = shard.shape[-1]
+    span = left.shape[-1] // side
+    for i in range(TB):
+        for k in range(span):
+            slot = table[entry, i * span + k]
+            first = pl.multiple_of(jnp.maximum(slot, 0) * height, height)
+            tile = shard[pl.ds(first, height), :]
+            left[i * height : (i + 1) * height, k * side : (k + 1) * side] = jnp.where(
+                slot >= 0, tile, jnp.zeros_like(tile)
+            )
+
+
+def block_of(left, table, entry, tiles, span, first):
+    right = jnp.concatenate(
+        [
+            jnp.concatenate([tiles[table[entry, k * TBC + first + j]] for j in range(WIDE)], axis=1)
+            for k in range(span)
+        ],
+        axis=0,
+    )
+    return jnp.dot(left[...], right, preferred_element_type=jnp.float32)
+
+
+def put_block(grid, first, value):
+    side = grid.shape[-1]
+    for j in range(WIDE):
+        grid[first + j] = value[:, j * side : (j + 1) * side]
+
+
+def pick(out, grid, table, entry, first, before=None):
+    height = out.shape[-2]
+    for o in range(out.shape[0]):
+        place = table[entry, first + o]
+        tile = grid[place % TBC, pl.ds(pl.multiple_of((place // TBC) * height, height), height), :]
+        out[o] = tile if before is None else tile + before[o]
+
+
+def slot_table(place, count, cells):
+    slot = jnp.arange(place.shape[-1], dtype=jnp.int32)
+    hit = (place[:, :, None] == jnp.arange(cells, dtype=jnp.int32)) & (
+        slot[None, :, None] < count[:, None, None]
+    )
+    return jnp.sum(jnp.where(hit, slot[None, :, None] + 1, 0), axis=1) - 1
+
+
+def note_rows(dtype, side, *numbers):
+    note = jnp.concatenate([n.reshape(-1) for n in numbers])
+    note = jnp.pad(note, (0, side - note.size)).astype(dtype)
+    return jnp.broadcast_to(note, (16, side))
+
+
+def note_of(shard):
+    return shard[-1].astype(jnp.int32)
+
+
+def widen(rows, side):
+    return jnp.pad(rows, ((0, 0), (0, side - rows.shape[-1])))
+
+
+def planned_shards(a_tiles, a_place, a_count, b_tiles, b_place, b_count, out_place):
+    side = a_tiles.shape[-1]
+    na, nb, no = a_place.shape[-1], b_place.shape[-1], out_place.shape[-1]
+    row, col, layer = (lax.axis_index(n).astype(jnp.int32) for n in ("row", "col", "layer"))
+    span, half, low = KL // 4, no // 2, side // 2
+    inner = span * side
+
+    b = b_tiles.reshape(nb, side, side)
+    b_x, b_y = flip(b, 1), flip(b, 2)
+    a_note = note_rows(a_tiles.dtype, side, a_place, a_count)
+    a = jnp.concatenate([a_tiles.reshape(na * side, side), a_note])
+    cut = na * side // 2
+    two = jnp.concatenate(
+        [across(g, "col", [(c, c ^ 2) for c in range(4)]) for g in (a[:cut], a[cut:])]
+    )
+    one = across(a, "col", [(c, c ^ 1) for c in range(4)])
+    b_note = jnp.concatenate([b_place.reshape(-1), b_count.reshape(-1), out_place.reshape(-1)])
+    b_note_x, b_note_y = flip(b_note, 1), flip(b_note, 2)
+    three = jnp.concatenate(
+        [across(g, "col", [(c, c ^ 1) for c in range(4)]) for g in (two[:cut], two[cut:])]
+    )
+    a_got = [a, one, two, three]
+    place = widen(jnp.stack([row, col, layer])[None], side)
+    a_notes = jnp.stack([note_of(g) for g in a_got])
+    lefts = jnp.stack(
+        [lax.dynamic_index_in_dim(a_notes, col ^ row ^ q, keepdims=False) for q in range(3)]
+    )
+    left_table = widen(slot_table(lefts[:, :na], lefts[:, na], TB * span), side)
+
+    def right_tables(notes):
+        table = slot_table(notes[:, :nb], notes[:, nb], span * TBC)
+        return jnp.where(table < 0, nb, table), widen(notes[:, nb + 1 :], side)
+
+
+    def load_rights(refs, tiles, sems):
+        copies = [
+            pltpu.make_async_copy(ref, tiles.at[n, 0:nb], sems.at[n]) for n, ref in enumerate(refs)
+        ]
+        for n, c in enumerate(copies):
+            c.start()
+            tiles[n, nb] = jnp.zeros((side, side), tiles.dtype)
+        return copies
+
+    def help_neighbours(
+        table, b_y, b_x, upper, lower, keep, give, left, total, tiles, sems, shards, shard_sems, note_v, note_s, slots
+    ):
+        near = [
+            pltpu.make_async_copy(ref, shards.at[q], shard_sems.at[q])
+            for q, ref in enumerate((upper, lower))
+        ]
+        for c in near:
+            c.start()
+        copies = load_rights((b_y, b_x), tiles, sems)
+        layer = table[4, 2]
+        for q in range(2):
+            near[q].wait()
+            note = shards[q, na * low :, :].astype(jnp.float32).astype(jnp.int32)
+            note_v[q] = note[: note_v.shape[1]]
+        noted = pltpu.make_async_copy(note_v, note_s, shard_sems.at[0])
+        noted.start()
+        noted.wait()
+        for q in range(2):
+            for cell in range(TB * span):
+                slots[q, cell] = -1
+            for slot in range(na):
+
+                @pl.when(slot < note_s[q, 0, na])
+                def _():
+                    slots[q, note_s[q, 0, slot]] = slot
+
+        for q in range(2):
+            rows_of(left.at[q], slots, q, shards.at[q], low)
+            copies[q].wait()
+            for first in range(0, TBC, WIDE):
+                part = block_of(left.at[q], table, q, tiles.at[q], span, first)
+                put_block(total.at[q], first, part)
+        for q in range(2):
+            pick(give.at[q], total.at[q], table, 2 + q, (1 - layer) * half)
+            pick(keep.at[q], total.at[q], table, 2 + q, layer * half)
+
+    def own_blocks(blocks):
+        def kernel(table, *refs):
+            lefts, refs = refs[0:4], refs[4:]
+            before, refs = refs[: 2 * (len(blocks) == 2)], refs[2 * (len(blocks) == 2) :]
+            rights, refs = refs[: len(blocks)], refs[len(blocks) :]
+            keep, give, left, total, tiles, sems = refs
+            copies = load_rights(rights, tiles, sems)
+            at = 2 * len(blocks) + 1
+            row, col, layer = (table[at, n] for n in range(3))
+            for e in range(4):
+                for n, q in enumerate(blocks):
+
+                    @pl.when((e ^ col ^ row) == q)
+                    def _():
+                        rows_of(left.at[n], table, n, lefts[e], side)
+
+            for c in copies:
+                c.wait()
+            for first in range(0, TBC, WIDE):
+                acc = None
+                for n in range(len(blocks)):
+                    part = block_of(left.at[n], table, len(blocks) + n, tiles.at[n], span, first)
+                    acc = part if acc is None else acc + part
+                put_block(total, first, acc)
+            pick(give, total, table, at - 1, (1 - layer) * half, before[1] if before else None)
+            pick(keep, total, table, at - 1, layer * half, before[0] if before else None)
+
+        return kernel
+
+    smem = pl.BlockSpec(memory_space=pltpu.SMEM)
+    vmem = pl.BlockSpec(memory_space=pltpu.VMEM)
+    hbm = pl.BlockSpec(memory_space=pltpu.HBM)
+
+    def call(kernel, name, table, near, rights, out, height, grids, far=()):
+        return pl.pallas_call(
+            kernel,
+            in_specs=[smem] + [vmem] * len(near) + [hbm] * len((*rights, *far)),
+            out_specs=(vmem, vmem),
+            out_shape=(out, out),
+            scratch_shapes=[
+                pltpu.VMEM((len(rights), TB * height, inner), a.dtype),
+                pltpu.VMEM(grids + (TBC, TB * height, side), jnp.float32),
+                pltpu.VMEM((len(rights), nb + 1, side, side), b.dtype),
+                pltpu.SemaphoreType.DMA((len(rights),)),
+            ]
+            + [pltpu.VMEM((len(far), *g.shape), g.dtype) for g in far[:1]]
+            + [pltpu.SemaphoreType.DMA((len(far),)) for g in far[:1]]
+            + [pltpu.VMEM((len(far), 8, side), jnp.int32) for g in far[:1]]
+            + [pltpu.SMEM((len(far), 8, side), jnp.int32) for g in far[:1]]
+            + [pltpu.SMEM((len(far), TB * span), jnp.int32) for g in far[:1]],
+            compiler_params=pltpu.CompilerParams(vmem_limit_bytes=2**21
+                + 2 * len(rights) * (TB * height * inner + (nb + 1) * side * side)
+                + 4 * TBC * TB * height * side * max(1, len(grids) * 2)),
+            cost_estimate=pl.CostEstimate(
+                flops=2 * len(rights) * TB * height * inner * TBC * side,
+                bytes_accessed=sum(g.size for g in rights) * 2,
+                transcendentals=0,
+            ),
+            name=name,
+        )(table, *near, *rights, *far)
+
+    whole = jax.ShapeDtypeStruct((half, side, side), jnp.float32)
+    spare = lax.select_n(col ^ row ^ 3, *a_got)
+    tiles = spare[: na * side].reshape(na, side, side)
+    upper, lower = (
+        jnp.concatenate([g.reshape(na * low, side), spare[na * side :]])
+        for g in (tiles[:, :low], tiles[:, low:])
+    )
+    upper, lower = flip(upper, 1), flip(lower, 2)
+
+    own_table, pattern = right_tables(b_note[None])
+    own_table = jnp.concatenate([left_table[:1], own_table, pattern, place])
+    keep, give = call(own_blocks((0,)), "own_block", own_table, a_got, (b,), whole, side, ())
+    a_got, b_x, b_y, b_note_x, b_note_y, keep, give = lax.optimization_barrier(
+        (a_got, b_x, b_y, b_note_x, b_note_y, keep, give)
+    )
+    right_table, patterns = right_tables(jnp.stack([b_note_x, b_note_y]))
+    table = jnp.concatenate([left_table[1:], right_table, pattern, place])
+    keep, give = call(
+        own_blocks((1, 2)), "near_blocks", table, (*a_got, keep, give), (b_x, b_y), whole, side, ()
+    )
+    upper, lower, keep, give = lax.optimization_barrier((upper, lower, keep, give))
+    table = jnp.concatenate([right_table[1:], right_table[:1], patterns, place])
+    part = jax.ShapeDtypeStruct((2, half, low, side), jnp.float32)
+    part_keep, part_give = call(
+        help_neighbours, "help_neighbours", table, (), (b_y, b_x), part, low, (2,), (upper, lower)
+    )
+    part_other = swap_layers(part_give)
+    other = swap_layers(give)
+    steps = half * low
+
+    def encode(keep, other, *codes):
+        for q, code in enumerate(codes):
+            values = [keep[q, o] + other[q, o] for o in range(half)]
+            tops = [jnp.max(jnp.abs(v), axis=0, keepdims=True) for v in values]
+            top = jnp.maximum(jnp.concatenate(tops, axis=0), 1e-30)
+            exponent = jnp.ceil(jnp.log2(top))
+            scale = jnp.exp2(15.0 - exponent)
+            for o, value in enumerate(values):
+                value = jnp.clip(value * scale[o : o + 1, :], -32767.0, 32767.0)
+                value = jnp.round(value).astype(jnp.int32)
+                code[o * low : (o + 1) * low, :] = value.astype(jnp.int16)
+            code[steps:, :] = exponent.astype(jnp.int32).astype(jnp.int16)
+
+    def finish(keep, other, from_x, from_y, out):
+        for q, code in enumerate((from_x, from_y)):
+            step = jnp.exp2(code[steps:, :].astype(jnp.int32).astype(jnp.float32) - 15.0)
+            for o in range(half):
+                at = (o, slice(q * low, (q + 1) * low), slice(None))
+                part = code[o * low : (o + 1) * low, :].astype(jnp.int32).astype(jnp.float32)
+                out[at] = (keep[at] + other[at] + part * step[o : o + 1, :]).astype(out.dtype)
+
+    code = jax.ShapeDtypeStruct((steps + half, side), jnp.int16)
+    code_x, code_y = pl.pallas_call(
+        encode, in_specs=[vmem] * 2, out_specs=(vmem, vmem), out_shape=(code, code), name="encode",
+        compiler_params=pltpu.CompilerParams(vmem_limit_bytes=4 * 2**20),
+    )(part_keep, part_other)
+    from_x, from_y = flip(code_x, 1), flip(code_y, 2)
+    result = pl.pallas_call(
+        finish,
+        in_specs=[vmem] * 4,
+        out_specs=vmem,
+        out_shape=jax.ShapeDtypeStruct((half, side, side), jnp.bfloat16),
+        name="finish",
+        compiler_params=pltpu.CompilerParams(vmem_limit_bytes=4 * 2**20),
+    )(keep, other, from_x, from_y)
+    return result.reshape(1, 1, half, side, side)
+
+
 def solution(mesh):
+    if mesh.shape["row"] == 4 and mesh.shape["col"] == 4:
+        body = planned_shards
+    else:
+        body = gathered_shards
     return jax.shard_map(
-        shards,
+        body,
         mesh=mesh,
         in_specs=(
             P("row", "layer", "col", None, None, None),

time: 217 us -> 78.6 us (0.36)
  waiting for transfers between devices: 89.9 us -> 35.2 us
  blocking collectives: 49.7 us -> 0 us
  matrix products: 38.5 us -> 0 us
  local copies, waits for them, and re-layouts: 21.3 us -> 3.49 us
  Pallas kernels: 0 us -> 17.1 us
  starting transfers between devices: 0.04 us -> 16.6 us
  between operations: 14.8 us -> 1.59 us
  other arithmetic: 2.1 us -> 4.3 us
    all_gather x2 -> x0, waiting for transfers between devices: 88.5 us -> none  [the longest x1 81.9 us: shards(): lax.all_gather(b_tiles, 'row', axis=1, tiled=True)]
    dot_general x3 -> x0, matrix products: 38.5 us -> none  [the longest x1 23.6 us: tile_product(): jnp.einsum('ikab,kjbc->iajc', left_grid, right_grid, preferred_element_ty...]
    ppermute x0 -> x15, waiting for transfers between devices: none -> 35.2 us  [across(): return lax.ppermute(x, axes, pairs)]
    unnamed x2 -> x0, blocking collectives: 18 us -> none
    pallas_call x0 -> x5, Pallas kernels: none -> 17.1 us  [the longest x3 15.7 us: call(): pl.pallas_call(kernel, in_specs=[smem] + [vmem] * len(near) + [hbm] * len...]
    all_gather x2 -> x0, blocking collectives: 16.8 us -> none  [the longest x1 8.95 us: shards(): lax.all_gather(a_place, 'col', axis=2, tiled=True)]
    ppermute x0 -> x15, starting transfers between devices: none -> 16.6 us  [across(): return lax.ppermute(x, axes, pairs)]
    all_gather x3 -> x0, local copies, waits for them, and re-layouts: 15.5 us -> none  [the longest x1 12 us: shards(): lax.all_gather(b_tiles, 'row', axis=1, tiled=True)]
  transfers between devices with their start and end apart: 2 -> 15, of which waited for: 2 -> 6; matrix products, arithmetic and copies ran while one was open for 6% -> 9% of each run, Pallas kernels for 0% -> 14%
where the time goes in v2:
time: 78.6 us; the launch traced here: 78.3 us
  waiting for transfers between devices  35.2 us (45%)
  Pallas kernels  17.1 us (22%)
  starting transfers between devices  16.6 us (21%)
  other arithmetic  4.3 us (5%)
  local copies, waits for them, and re-layouts  3.49 us (4%)
  between operations  1.59 us (2%)
    ppermute x15, waiting for transfers between devices, across(): return lax.ppermute(x, axes, pairs)  35.2 us
    ppermute x15, starting transfers between devices, across(): return lax.ppermute(x, axes, pairs)  16.6 us
    pallas_call x3, Pallas kernels, call(): pl.pallas_call(kernel, in_specs=[smem] + [vmem] * len(near) + [hbm] * len...  15.7 us
    concatenate x2, other arithmetic, planned_shards(): a = jnp.concatenate([a_tiles.reshape(na * side, side), a_note])  1.83 us
  transfers between devices with their start and end apart: 15, of which 6 were waited for; matrix products, arithmetic and copies ran while one was open for 9% of the time, Pallas kernels for 14%

profile of v2, /device:TPU:0, one launch (start us, length us, event | category | flops | bytes accessed | tf_op | source)
XLA Modules:
  0.0 78.3 jit_solution(17292497401062098903)
XLA Ops:
  0.0 2.9 %collective-permute-start.7 = (bf16[64,128,128]{2,1,0:T(8,128)(2,1)}, bf16[64,128,128]{2,1,0:T(8,128)(2,1)S(1)}, u32[]{:S(2)}, u32[]{:S(2)}) collective-permute-start(bf16[64,128,128]{2,1,0:T(8,128)(2,1)} %bitcast.31), channel_id=1, source_target_pairs={{0,8},{8,0},{16,24},{24,16},{1,9},{9,1},{17,25},{25,17},{2,10},{10... | collective-permute-start | bytes 6291464 | tf_op jit(solution)/shard_map/ppermute | solution.py:71
  2.9 1.5 %collective-permute-start.8 = (bf16[64,128,128]{2,1,0:T(8,128)(2,1)}, bf16[64,128,128]{2,1,0:T(8,128)(2,1)}, u32[]{:S(2)}, u32[]{:S(2)}) collective-permute-start(bf16[64,128,128]{2,1,0:T(8,128)(2,1)} %bitcast.32), channel_id=1, source_target_pairs={{0,16},{8,24},{16,0},{24,8},{1,17},{9,25},{17,1},{25,9},{2,18},{10... | collective-permute-start | bytes 6291464 | tf_op jit(solution)/shard_map/ppermute | solution.py:71
  5.1 0.7 convert_bitcast_fusion
  5.9 1.1 %pad_maximum_fusion.refs_0_ = bf16[2064,128]{1,0:T(8,128)(2,1)S(1)} fusion(bf16[16,128]{1,0:T(8,128)(2,1)S(1)} %broadcast_in_dim.65, bf16[2048,128]{1,0:T(8,128)(2,1)} %bitcast.34), kind=kLoop, calls=%fused_computation.1 | loop fusion | flops 1056768 | bytes 1056768 | tf_op jit(solution)/shard_map/concatenate | solution.py:152
  7.0 1.6 %collective-permute-start = (bf16[2064,128]{1,0:T(8,128)(2,1)S(1)}, bf16[2064,128]{1,0:T(8,128)(2,1)S(1)}, u32[]{:S(2)}, u32[]{:S(2)}) collective-permute-start(bf16[2064,128]{1,0:T(8,128)(2,1)S(1)} %pad_maximum_fusion.refs_0_), channel_id=1, source_target_pairs={{0,2},{2,0},{4,6},{6,4},{1,3},{3,1},{5,7},{7,5},{8,10},{10,8},{12,... | collective-permute-start | bytes 1585160 | tf_op jit(solution)/shard_map/ppermute | solution.py:71
  8.6 0.7 fusion
  9.3 2.6 %collective-permute-start.2 = (bf16[1040,128]{1,0:T(8,128)(2,1)}, bf16[1040,128]{1,0:T(8,128)(2,1)S(1)}, u32[]{:S(2)}, u32[]{:S(2)}) collective-permute-start(bf16[1040,128]{1,0:T(8,128)(2,1)} %fusion), channel_id=1, source_target_pairs={{0,4},{2,6},{4,0},{6,2},{1,5},{3,7},{5,1},{7,3},{8,12},{10,14},{12... | collective-permute-start | bytes 798728 | tf_op jit(solution)/shard_map/ppermute | solution.py:71
  11.9 0.7 slice.74
  12.6 0.3 collective-permute-start.1
  13.7 0.6 slice.91
  14.3 0.6 iota_compare_fusion.5
  15.3 19.6 %collective-permute-done.1 = bf16[1024,128]{1,0:T(8,128)(2,1)} collective-permute-done((bf16[1024,128]{1,0:T(8,128)(2,1)}, bf16[1024,128]{1,0:T(8,128)(2,1)}, u32[]{:S(2)}, u32[]{:S(2)}) %collective-permute-start.1) | collective-permute-done | bytes 262176 | tf_op jit(solution)/shard_map/ppermute | solution.py:71
  34.9 1.0 %constant_dynamic-update-slice_fusion.1 = bf16[2064,128]{1,0:T(8,128)(2,1)S(1)} fusion(bf16[1024,128]{1,0:T(8,128)(2,1)} %collective-permute-done.1), kind=kLoop, calls=%fused_computation.17 | loop fusion | bytes 524288
  36.0 2.1 %collective-permute-start.4 = (bf16[1040,128]{1,0:T(8,128)(2,1)S(1)}, bf16[1040,128]{1,0:T(8,128)(2,1)S(1)}, u32[]{:S(2)}, u32[]{:S(2)}) collective-permute-start(bf16[1040,128]{1,0:T(8,128)(2,1)S(1)} %collective-permute-done.2), channel_id=1, source_target_pairs={{0,2},{2,0},{4,6},{6,4},{1,3},{3,1},{5,7},{7,5},{8,10},{10,8},{12,... | collective-permute-start | bytes 798728 | tf_op jit(solution)/shard_map/ppermute | solution.py:71
  38.1 5.1 %collective-permute-done.3 = bf16[1024,128]{1,0:T(8,128)(2,1)S(1)} collective-permute-done((bf16[1024,128]{1,0:T(8,128)(2,1)}, bf16[1024,128]{1,0:T(8,128)(2,1)S(1)}, u32[]{:S(2)}, u32[]{:S(2)}) %collective-permute-start.3) | collective-permute-done | bytes 262176 | tf_op jit(solution)/shard_map/ppermute | solution.py:71
  43.2 0.5 collective-permute-start.10
  43.7 0.6 collective-permute-start.9
  44.3 1.7 %collective-permute-done.4 = bf16[1040,128]{1,0:T(8,128)(2,1)S(1)} collective-permute-done((bf16[1040,128]{1,0:T(8,128)(2,1)S(1)}, bf16[1040,128]{1,0:T(8,128)(2,1)S(1)}, u32[]{:S(2)}, u32[]{:S(2)}) %collective-permute-start.4) | collective-permute-done | bytes 266272 | tf_op jit(solution)/shard_map/ppermute | solution.py:71
  46.5 0.6 collective-permute-start.5
  47.6 0.4 copy-done
  48.0 3.5 %own_block.1 = (f32[16,128,128]{2,1,0:T(8,128)S(1)}, f32[16,128,128]{2,1,0:T(8,128)S(1)}) custom-call(s32[4,128]{1,0:T(4,128)S(1)} %pad_add_fusion.3.table, bf16[2064,128]{1,0:T(8,128)(2,1)S(1)} %pad_maximum_fusion.refs_0_, bf16[2064,128]{1,0:T(8,128)(2,1)S(1)} %collective-permute-done.refs_1_, ...), custom_call_target="tpu_custom_call" | custom-call | flops 2147483648 | bytes 2097152 | tf_op jit(solution)/shard_map/own_block/pallas_call | solution.py:256
  51.6 0.6 collective-permute-start.6
  52.6 7.1 %near_blocks.1 = (f32[16,128,128]{2,1,0:T(8,128)S(1)}, f32[16,128,128]{2,1,0:T(8,128)S(1)}) custom-call(s32[6,128]{1,0:T(8,128)S(1)} %pad_add_fusion.1.table, bf16[2064,128]{1,0:T(8,128)(2,1)S(1)} %pad_maximum_fusion.refs_0_, bf16[2064,128]{1,0:T(8,128)(2,1)S(1)} %collective-permute-done.refs_1_, ...), custom_call_target="tpu_custom_call" | custom-call | flops 4294967296 | bytes 4194304 | tf_op jit(solution)/shard_map/near_blocks/pallas_call | solution.py:256
  59.8 5.1 %help_neighbours.1 = (f32[2,16,64,128]{3,2,1,0:T(8,128)S(1)}, f32[2,16,64,128]{3,2,1,0:T(8,128)S(1)}) custom-call(s32[5,128]{1,0:T(8,128)S(1)} %fusion.4.table, bf16[64,128,128]{2,1,0:T(8,128)(2,1)} %collective-permute-done.8.refs_7_.b_y, bf16[64,128,128]{2,1,0:T(8,128)(2,1)S(1)} %collective-permute-done.7.refs_6_.b_x, ...), custom_call_target="tpu_custom_call" | custom-call | flops 2147483648 | bytes 4194304 | tf_op jit(solution)/shard_map/help_neighbours/pallas_call | solution.py:256
  65.0 0.5 collective-permute-start.11
  65.5 2.1 %collective-permute-done.12.other = f32[2,16,64,128]{3,2,1,0:T(8,128)S(1)} collective-permute-done((f32[2,16,64,128]{3,2,1,0:T(8,128)S(1)}, f32[2,16,64,128]{3,2,1,0:T(8,128)S(1)}, u32[]{:S(2)}, u32[]{:S(2)}) %collective-permute-start.12) | collective-permute-done | bytes 1048608 | tf_op jit(solution)/shard_map/ppermute | solution.py:71
  67.6 0.3 encode.1
  67.9 1.1 %collective-permute-start.13 = (s16[1040,128]{1,0:T(8,128)(2,1)S(1)}, s16[1040,128]{1,0:T(8,128)(2,1)S(1)}, u32[]{:S(2)}, u32[]{:S(2)}) collective-permute-start(s16[1040,128]{1,0:T(8,128)(2,1)S(1)} %get-tuple-element.47), channel_id=1, source_target_pairs={{0,8},{8,0},{16,24},{24,16},{1,9},{9,1},{17,25},{25,17},{2,10},{10... | collective-permute-start | bytes 798728 | tf_op jit(solution)/shard_map/ppermute | solution.py:71
  69.1 1.5 %collective-permute-start.14 = (s16[1040,128]{1,0:T(8,128)(2,1)S(1)}, s16[1040,128]{1,0:T(8,128)(2,1)S(1)}, u32[]{:S(2)}, u32[]{:S(2)}) collective-permute-start(s16[1040,128]{1,0:T(8,128)(2,1)S(1)} %get-tuple-element.48), channel_id=1, source_target_pairs={{0,16},{8,24},{16,0},{24,8},{1,17},{9,25},{17,1},{25,9},{2,18},{10... | collective-permute-start | bytes 798728 | tf_op jit(solution)/shard_map/ppermute | solution.py:71
  70.6 5.8 %collective-permute-done.13.from_x = s16[1040,128]{1,0:T(8,128)(2,1)S(1)} collective-permute-done((s16[1040,128]{1,0:T(8,128)(2,1)S(1)}, s16[1040,128]{1,0:T(8,128)(2,1)S(1)}, u32[]{:S(2)}, u32[]{:S(2)}) %collective-permute-start.13) | collective-permute-done | bytes 266272 | tf_op jit(solution)/shard_map/ppermute | solution.py:71
  76.4 0.8 %collective-permute-done.14.from_y = s16[1040,128]{1,0:T(8,128)(2,1)S(1)} collective-permute-done((s16[1040,128]{1,0:T(8,128)(2,1)S(1)}, s16[1040,128]{1,0:T(8,128)(2,1)S(1)}, u32[]{:S(2)}, u32[]{:S(2)}) %collective-permute-start.14) | collective-permute-done | bytes 266272 | tf_op jit(solution)/shard_map/ppermute | solution.py:71
  77.2 1.0 %finish.1 = bf16[16,128,128]{2,1,0:T(8,128)(2,1)} custom-call(f32[16,128,128]{2,1,0:T(8,128)S(1)} %get-tuple-element.41.keep, f32[16,128,128]{2,1,0:T(8,128)S(1)} %collective-permute-done.11.other, s16[1040,128]{1,0:T(8,128)(2,1)S(1)} %collective-permute-done.13.from_x, s16[1040,128]{1,0:T(8,128)(2,1)S(1)} %collective-permute-done.14.from_y), custom_call_target="tpu_custom_call" | custom-call | tf_op jit(solution)/shard_map/finish/pallas_call | solution.py:340
  (63 shorter events, 2.1 us)
Async XLA Ops:
  0.0 8.6 %copy-start.1 = (bf16[1,1,1,16,128,128]{5,4,3,2,1,0:T(8,128)(2,1)S(1)}, bf16[1,1,1,16,128,128]{5,4,3,2,1,0:T(8,128)(2,1)}, u32[]{:S(2)}) copy-start(bf16[1,1,1,16,128,128]{5,4,3,2,1,0:T(8,128)(2,1)} %param.7) | copy-start | bytes 1572868
  0.0 52.2 %collective-permute-start.7 = (bf16[64,128,128]{2,1,0:T(8,128)(2,1)}, bf16[64,128,128]{2,1,0:T(8,128)(2,1)S(1)}, u32[]{:S(2)}, u32[]{:S(2)}) collective-permute-start(bf16[64,128,128]{2,1,0:T(8,128)(2,1)} %bitcast.31), channel_id=1, source_target_pairs={{0,8},{8,0},{16,24},{24,16},{1,9},{9,1},{17,25},{25,17},{2,10},{10... | collective-permute-start | bytes 6291464 | tf_op jit(solution)/shard_map/ppermute | solution.py:71
  2.9 49.2 %collective-permute-start.8 = (bf16[64,128,128]{2,1,0:T(8,128)(2,1)}, bf16[64,128,128]{2,1,0:T(8,128)(2,1)}, u32[]{:S(2)}, u32[]{:S(2)}) collective-permute-start(bf16[64,128,128]{2,1,0:T(8,128)(2,1)} %bitcast.32), channel_id=1, source_target_pairs={{0,16},{8,24},{16,0},{24,8},{1,17},{9,25},{17,1},{25,9},{2,18},{10... | collective-permute-start | bytes 6291464 | tf_op jit(solution)/shard_map/ppermute | solution.py:71
  5.9 7.8 %copy-start.3 = (s32[1,1,32]{2,1,0:T(1,128)S(1)}, s32[1,1,32]{2,1,0:T(1,128)}, u32[]{:S(2)}) copy-start(s32[1,1,32]{2,1,0:T(1,128)} %param.13) | copy-start | bytes 388
  5.9 7.8 %copy-start.4 = (s32[1,1,1,64]{3,2,1,0:T(1,128)S(1)}, s32[1,1,1,64]{3,2,1,0:T(1,128)}, u32[]{:S(2)}) copy-start(s32[1,1,1,64]{3,2,1,0:T(1,128)} %param.11) | copy-start | bytes 772
  7.0 36.8 %collective-permute-start = (bf16[2064,128]{1,0:T(8,128)(2,1)S(1)}, bf16[2064,128]{1,0:T(8,128)(2,1)S(1)}, u32[]{:S(2)}, u32[]{:S(2)}) collective-permute-start(bf16[2064,128]{1,0:T(8,128)(2,1)S(1)} %pad_maximum_fusion.refs_0_), channel_id=1, source_target_pairs={{0,2},{2,0},{4,6},{6,4},{1,3},{3,1},{5,7},{7,5},{8,10},{10,8},{12,... | collective-permute-start | bytes 1585160 | tf_op jit(solution)/shard_map/ppermute | solution.py:71
  9.3 26.6 %collective-permute-start.2 = (bf16[1040,128]{1,0:T(8,128)(2,1)}, bf16[1040,128]{1,0:T(8,128)(2,1)S(1)}, u32[]{:S(2)}, u32[]{:S(2)}) collective-permute-start(bf16[1040,128]{1,0:T(8,128)(2,1)} %fusion), channel_id=1, source_target_pairs={{0,4},{2,6},{4,0},{6,2},{1,5},{3,7},{5,1},{7,3},{8,12},{10,14},{12... | collective-permute-start | bytes 798728 | tf_op jit(solution)/shard_map/ppermute | solution.py:71
  12.6 22.3 %collective-permute-start.1 = (bf16[1024,128]{1,0:T(8,128)(2,1)}, bf16[1024,128]{1,0:T(8,128)(2,1)}, u32[]{:S(2)}, u32[]{:S(2)}) collective-permute-start(bf16[1024,128]{1,0:T(8,128)(2,1)} %bitcast.3), channel_id=1, source_target_pairs={{0,4},{2,6},{4,0},{6,2},{1,5},{3,7},{5,1},{7,3},{8,12},{10,14},{12... | collective-permute-start | bytes 786440 | tf_op jit(solution)/shard_map/ppermute | solution.py:71
  15.3 30.8 %copy-start.2 = (bf16[1,1,1,16,128,128]{5,4,3,2,1,0:T(8,128)(2,1)S(1)}, bf16[1,1,1,16,128,128]{5,4,3,2,1,0:T(8,128)(2,1)}, u32[]{:S(2)}) copy-start(bf16[1,1,1,16,128,128]{5,4,3,2,1,0:T(8,128)(2,1)} %param.7) | copy-start | bytes 1572868
  34.9 8.3 %collective-permute-start.3 = (bf16[1024,128]{1,0:T(8,128)(2,1)}, bf16[1024,128]{1,0:T(8,128)(2,1)S(1)}, u32[]{:S(2)}, u32[]{:S(2)}) collective-permute-start(bf16[1024,128]{1,0:T(8,128)(2,1)} %collective-permute-done.1), channel_id=1, source_target_pairs={{0,2},{2,0},{4,6},{6,4},{1,3},{3,1},{5,7},{7,5},{8,10},{10,8},{12,... | collective-permute-start | bytes 786440 | tf_op jit(solution)/shard_map/ppermute | solution.py:71
  36.0 10.1 %collective-permute-start.4 = (bf16[1040,128]{1,0:T(8,128)(2,1)S(1)}, bf16[1040,128]{1,0:T(8,128)(2,1)S(1)}, u32[]{:S(2)}, u32[]{:S(2)}) collective-permute-start(bf16[1040,128]{1,0:T(8,128)(2,1)S(1)} %collective-permute-done.2), channel_id=1, source_target_pairs={{0,2},{2,0},{4,6},{6,4},{1,3},{3,1},{5,7},{7,5},{8,10},{10,8},{12,... | collective-permute-start | bytes 798728 | tf_op jit(solution)/shard_map/ppermute | solution.py:71
  43.2 8.4 %collective-permute-start.10 = (s32[97]{0:T(128)S(1)}, s32[97]{0:T(128)S(1)}, u32[]{:S(2)}, u32[]{:S(2)}) collective-permute-start(s32[97]{0:T(128)S(1)} %pad_add_fusion.5), channel_id=1, source_target_pairs={{0,16},{8,24},{16,0},{24,8},{1,17},{9,25},{17,1},{25,9},{2,18},{10... | collective-permute-start | bytes 1172 | tf_op jit(solution)/shard_map/ppermute | solution.py:71
  43.7 8.4 %collective-permute-start.9 = (s32[97]{0:T(128)S(1)}, s32[97]{0:T(128)S(1)}, u32[]{:S(2)}, u32[]{:S(2)}) collective-permute-start(s32[97]{0:T(128)S(1)} %pad_add_fusion.5), channel_id=1, source_target_pairs={{0,8},{8,0},{16,24},{24,16},{1,9},{9,1},{17,25},{25,17},{2,10},{10... | collective-permute-start | bytes 1172 | tf_op jit(solution)/shard_map/ppermute | solution.py:71
  46.4 1.6 %copy-start = (bf16[1,1,1,64,128,128]{5,4,3,2,1,0:T(8,128)(2,1)S(1)}, bf16[1,1,1,64,128,128]{5,4,3,2,1,0:T(8,128)(2,1)}, u32[]{:S(2)}) copy-start(bf16[1,1,1,64,128,128]{5,4,3,2,1,0:T(8,128)(2,1)} %param.10) | copy-start | bytes 6291460
  46.5 13.3 %collective-permute-start.5 = (bf16[1040,128]{1,0:T(8,128)(2,1)S(1)}, bf16[1040,128]{1,0:T(8,128)(2,1)S(1)}, u32[]{:S(2)}, u32[]{:S(2)}) collective-permute-start(bf16[1040,128]{1,0:T(8,128)(2,1)S(1)} %get-tuple-element.52), channel_id=1, source_target_pairs={{0,8},{8,0},{16,24},{24,16},{1,9},{9,1},{17,25},{25,17},{2,10},{10... | collective-permute-start | bytes 798728 | tf_op jit(solution)/shard_map/ppermute | solution.py:71
  51.6 8.2 %collective-permute-start.6 = (bf16[1040,128]{1,0:T(8,128)(2,1)S(1)}, bf16[1040,128]{1,0:T(8,128)(2,1)S(1)}, u32[]{:S(2)}, u32[]{:S(2)}) collective-permute-start(bf16[1040,128]{1,0:T(8,128)(2,1)S(1)} %get-tuple-element.51), channel_id=1, source_target_pairs={{0,16},{8,24},{16,0},{24,8},{1,17},{9,25},{17,1},{25,9},{2,18},{10... | collective-permute-start | bytes 798728 | tf_op jit(solution)/shard_map/ppermute | solution.py:71
  64.9 2.7 %collective-permute-start.12 = (f32[2,16,64,128]{3,2,1,0:T(8,128)S(1)}, f32[2,16,64,128]{3,2,1,0:T(8,128)S(1)}, u32[]{:S(2)}, u32[]{:S(2)}) collective-permute-start(f32[2,16,64,128]{3,2,1,0:T(8,128)S(1)} %get-tuple-element.46), channel_id=1, source_target_pairs={{0,1},{1,0},{2,3},{3,2},{4,5},{5,4},{6,7},{7,6},{8,9},{9,8},{10,11... | collective-permute-start | bytes 3145736 | tf_op jit(solution)/shard_map/ppermute | solution.py:71
  65.0 5.6 %collective-permute-start.11 = (f32[16,128,128]{2,1,0:T(8,128)S(1)}, f32[16,128,128]{2,1,0:T(8,128)S(1)}, u32[]{:S(2)}, u32[]{:S(2)}) collective-permute-start(f32[16,128,128]{2,1,0:T(8,128)S(1)} %get-tuple-element.42), channel_id=1, source_target_pairs={{0,1},{1,0},{2,3},{3,2},{4,5},{5,4},{6,7},{7,6},{8,9},{9,8},{10,11... | collective-permute-start | bytes 3145736 | tf_op jit(solution)/shard_map/ppermute | solution.py:71
  67.9 8.5 %collective-permute-start.13 = (s16[1040,128]{1,0:T(8,128)(2,1)S(1)}, s16[1040,128]{1,0:T(8,128)(2,1)S(1)}, u32[]{:S(2)}, u32[]{:S(2)}) collective-permute-start(s16[1040,128]{1,0:T(8,128)(2,1)S(1)} %get-tuple-element.47), channel_id=1, source_target_pairs={{0,8},{8,0},{16,24},{24,16},{1,9},{9,1},{17,25},{25,17},{2,10},{10... | collective-permute-start | bytes 798728 | tf_op jit(solution)/shard_map/ppermute | solution.py:71
  69.1 8.2 %collective-permute-start.14 = (s16[1040,128]{1,0:T(8,128)(2,1)S(1)}, s16[1040,128]{1,0:T(8,128)(2,1)S(1)}, u32[]{:S(2)}, u32[]{:S(2)}) collective-permute-start(s16[1040,128]{1,0:T(8,128)(2,1)S(1)} %get-tuple-element.48), channel_id=1, source_target_pairs={{0,16},{8,24},{16,0},{24,8},{1,17},{9,25},{17,1},{25,9},{2,18},{10... | collective-permute-start | bytes 798728 | tf_op jit(solution)/shard_map/ppermute | solution.py:71

commit v3 on v2

--- a/solution.py
+++ b/solution.py
@@ -151,15 +151,12 @@
     a_note = note_rows(a_tiles.dtype, side, a_place, a_count)
     a = jnp.concatenate([a_tiles.reshape(na * side, side), a_note])
     cut = na * side // 2
-    two = jnp.concatenate(
-        [across(g, "col", [(c, c ^ 2) for c in range(4)]) for g in (a[:cut], a[cut:])]
-    )
+    two = [across(g, "col", [(c, c ^ 2) for c in range(4)]) for g in (a[:cut], a[cut:])]
     one = across(a, "col", [(c, c ^ 1) for c in range(4)])
     b_note = jnp.concatenate([b_place.reshape(-1), b_count.reshape(-1), out_place.reshape(-1)])
     b_note_x, b_note_y = flip(b_note, 1), flip(b_note, 2)
-    three = jnp.concatenate(
-        [across(g, "col", [(c, c ^ 1) for c in range(4)]) for g in (two[:cut], two[cut:])]
-    )
+    three = [across(g, "col", [(c, c ^ 1) for c in range(4)]) for g in two]
+    two, three = jnp.concatenate(two), jnp.concatenate(three)
     a_got = [a, one, two, three]
     place = widen(jnp.stack([row, col, layer])[None], side)
     a_notes = jnp.stack([note_of(g) for g in a_got])
@@ -235,11 +232,11 @@
                     def _():
                         rows_of(left.at[n], table, n, lefts[e], side)
 
-            for c in copies:
-                c.wait()
             for first in range(0, TBC, WIDE):
                 acc = None
                 for n in range(len(blocks)):
+                    if first == 0:
+                        copies[n].wait()
                     part = block_of(left.at[n], table, len(blocks) + n, tiles.at[n], span, first)
                     acc = part if acc is None else acc + part
                 put_block(total, first, acc)
@@ -269,7 +266,7 @@
             + [pltpu.VMEM((len(far), 8, side), jnp.int32) for g in far[:1]]
             + [pltpu.SMEM((len(far), 8, side), jnp.int32) for g in far[:1]]
             + [pltpu.SMEM((len(far), TB * span), jnp.int32) for g in far[:1]],
-            compiler_params=pltpu.CompilerParams(vmem_limit_bytes=2**21
+            compiler_params=pltpu.CompilerParams(vmem_limit_bytes=5 * 2**20
                 + 2 * len(rights) * (TB * height * inner + (nb + 1) * side * side)
                 + 4 * TBC * TB * height * side * max(1, len(grids) * 2)),
             cost_estimate=pl.CostEstimate(
@@ -323,28 +320,43 @@
                 code[o * low : (o + 1) * low, :] = value.astype(jnp.int16)
             code[steps:, :] = exponent.astype(jnp.int32).astype(jnp.int16)
 
-    def finish(keep, other, from_x, from_y, out):
-        for q, code in enumerate((from_x, from_y)):
-            step = jnp.exp2(code[steps:, :].astype(jnp.int32).astype(jnp.float32) - 15.0)
-            for o in range(half):
+    def finish(mine, from_x, from_y, out, rounded, sems):
+        codes = (from_x, from_y)
+        scales = [jnp.exp2(c[steps:, :].astype(jnp.int32).astype(jnp.float32) - 15.0) for c in codes]
+        copies = []
+        for o in range(half):
+            for q in range(2):
                 at = (o, slice(q * low, (q + 1) * low), slice(None))
-                part = code[o * low : (o + 1) * low, :].astype(jnp.int32).astype(jnp.float32)
-                out[at] = (keep[at] + other[at] + part * step[o : o + 1, :]).astype(out.dtype)
+                part = codes[q][o * low : (o + 1) * low, :].astype(jnp.int32).astype(jnp.float32)
+                rounded[at] = (mine[at] + part * scales[q][o : o + 1, :]).astype(rounded.dtype)
+            if (o + 1) % (half // 4) == 0:
+                done = slice(o + 1 - half // 4, o + 1)
+                copies.append(
+                    pltpu.make_async_copy(rounded.at[done], out.at[done], sems.at[len(copies)])
+                )
+                copies[-1].start()
+        for c in copies:
+            c.wait()
 
     code = jax.ShapeDtypeStruct((steps + half, side), jnp.int16)
     code_x, code_y = pl.pallas_call(
         encode, in_specs=[vmem] * 2, out_specs=(vmem, vmem), out_shape=(code, code), name="encode",
-        compiler_params=pltpu.CompilerParams(vmem_limit_bytes=4 * 2**20),
+        compiler_params=pltpu.CompilerParams(vmem_limit_bytes=10 * 2**20),
     )(part_keep, part_other)
     from_x, from_y = flip(code_x, 1), flip(code_y, 2)
+    mine = keep + other
     result = pl.pallas_call(
         finish,
-        in_specs=[vmem] * 4,
-        out_specs=vmem,
+        in_specs=[vmem] * 3,
+        out_specs=hbm,
         out_shape=jax.ShapeDtypeStruct((half, side, side), jnp.bfloat16),
+        scratch_shapes=[
+            pltpu.VMEM((half, side, side), jnp.bfloat16),
+            pltpu.SemaphoreType.DMA((4,)),
+        ],
         name="finish",
-        compiler_params=pltpu.CompilerParams(vmem_limit_bytes=4 * 2**20),
-    )(keep, other, from_x, from_y)
+        compiler_params=pltpu.CompilerParams(vmem_limit_bytes=10 * 2**20),
+    )(mine, from_x, from_y)
     return result.reshape(1, 1, half, side, side)
 
 

time: 78.6 us -> 78.6 us (level)
  transfers between devices with their start and end apart: 15 -> 15, of which waited for: 6 -> 6; matrix products, arithmetic and copies ran while one was open for 9% -> 10% of each run, Pallas kernels for 14% -> 14%
where the time goes in v3:
time: 78.6 us; the launch traced here: 78.3 us
  waiting for transfers between devices  35.1 us (45%)
  Pallas kernels  16.9 us (22%)
  starting transfers between devices  16.6 us (21%)
  other arithmetic  4.44 us (6%)
  local copies, waits for them, and re-layouts  3.49 us (4%)
  between operations  1.76 us (2%)
    ppermute x15, waiting for transfers between devices, across(): return lax.ppermute(x, axes, pairs)  35.1 us
    ppermute x15, starting transfers between devices, across(): return lax.ppermute(x, axes, pairs)  16.6 us
    pallas_call x3, Pallas kernels, call(): pl.pallas_call(kernel, in_specs=[smem] + [vmem] * len(near) + [hbm] * len...  15.7 us
    concatenate x2, other arithmetic, planned_shards(): a = jnp.concatenate([a_tiles.reshape(na * side, side), a_note])  1.83 us
  transfers between devices with their start and end apart: 15, of which 6 were waited for; matrix products, arithmetic and copies ran while one was open for 10% of the time, Pallas kernels for 14%

profile of v3, /device:TPU:0, one launch (start us, length us, event | category | flops | bytes accessed | tf_op | source)
XLA Modules:
  0.0 78.3 jit_solution(7931724926777997864)
XLA Ops:
  0.0 2.9 %collective-permute-start.7 = (bf16[64,128,128]{2,1,0:T(8,128)(2,1)}, bf16[64,128,128]{2,1,0:T(8,128)(2,1)S(1)}, u32[]{:S(2)}, u32[]{:S(2)}) collective-permute-start(bf16[64,128,128]{2,1,0:T(8,128)(2,1)} %bitcast.31), channel_id=1, source_target_pairs={{0,8},{8,0},{16,24},{24,16},{1,9},{9,1},{17,25},{25,17},{2,10},{10... | collective-permute-start | bytes 6291464 | tf_op jit(solution)/shard_map/ppermute | solution.py:71
  2.9 1.5 %collective-permute-start.8 = (bf16[64,128,128]{2,1,0:T(8,128)(2,1)}, bf16[64,128,128]{2,1,0:T(8,128)(2,1)}, u32[]{:S(2)}, u32[]{:S(2)}) collective-permute-start(bf16[64,128,128]{2,1,0:T(8,128)(2,1)} %bitcast.32), channel_id=1, source_target_pairs={{0,16},{8,24},{16,0},{24,8},{1,17},{9,25},{17,1},{25,9},{2,18},{10... | collective-permute-start | bytes 6291464 | tf_op jit(solution)/shard_map/ppermute | solution.py:71
  5.1 0.7 convert_bitcast_fusion
  5.9 1.1 %pad_maximum_fusion.refs_0_ = bf16[2064,128]{1,0:T(8,128)(2,1)S(1)} fusion(bf16[16,128]{1,0:T(8,128)(2,1)S(1)} %broadcast_in_dim.65, bf16[2048,128]{1,0:T(8,128)(2,1)} %bitcast.34), kind=kLoop, calls=%fused_computation.1 | loop fusion | flops 1056768 | bytes 1056768 | tf_op jit(solution)/shard_map/concatenate | solution.py:152
  7.0 1.6 %collective-permute-start = (bf16[2064,128]{1,0:T(8,128)(2,1)S(1)}, bf16[2064,128]{1,0:T(8,128)(2,1)S(1)}, u32[]{:S(2)}, u32[]{:S(2)}) collective-permute-start(bf16[2064,128]{1,0:T(8,128)(2,1)S(1)} %pad_maximum_fusion.refs_0_), channel_id=1, source_target_pairs={{0,2},{2,0},{4,6},{6,4},{1,3},{3,1},{5,7},{7,5},{8,10},{10,8},{12,... | collective-permute-start | bytes 1585160 | tf_op jit(solution)/shard_map/ppermute | solution.py:71
  8.6 0.7 fusion
  9.3 2.6 %collective-permute-start.2 = (bf16[1040,128]{1,0:T(8,128)(2,1)}, bf16[1040,128]{1,0:T(8,128)(2,1)S(1)}, u32[]{:S(2)}, u32[]{:S(2)}) collective-permute-start(bf16[1040,128]{1,0:T(8,128)(2,1)} %fusion), channel_id=1, source_target_pairs={{0,4},{2,6},{4,0},{6,2},{1,5},{3,7},{5,1},{7,3},{8,12},{10,14},{12... | collective-permute-start | bytes 798728 | tf_op jit(solution)/shard_map/ppermute | solution.py:71
  11.9 0.7 slice.74
  12.6 0.3 collective-permute-start.1
  13.7 0.6 slice.91
  14.3 0.6 iota_compare_fusion.5
  15.3 19.6 %collective-permute-done.1 = bf16[1024,128]{1,0:T(8,128)(2,1)} collective-permute-done((bf16[1024,128]{1,0:T(8,128)(2,1)}, bf16[1024,128]{1,0:T(8,128)(2,1)}, u32[]{:S(2)}, u32[]{:S(2)}) %collective-permute-start.1) | collective-permute-done | bytes 262176 | tf_op jit(solution)/shard_map/ppermute | solution.py:71
  34.9 1.0 %constant_dynamic-update-slice_fusion.1 = bf16[2064,128]{1,0:T(8,128)(2,1)S(1)} fusion(bf16[1024,128]{1,0:T(8,128)(2,1)} %collective-permute-done.1), kind=kLoop, calls=%fused_computation.17 | loop fusion | bytes 524288
  36.0 2.1 %collective-permute-start.4 = (bf16[1040,128]{1,0:T(8,128)(2,1)S(1)}, bf16[1040,128]{1,0:T(8,128)(2,1)S(1)}, u32[]{:S(2)}, u32[]{:S(2)}) collective-permute-start(bf16[1040,128]{1,0:T(8,128)(2,1)S(1)} %collective-permute-done.2), channel_id=1, source_target_pairs={{0,2},{2,0},{4,6},{6,4},{1,3},{3,1},{5,7},{7,5},{8,10},{10,8},{12,... | collective-permute-start | bytes 798728 | tf_op jit(solution)/shard_map/ppermute | solution.py:71
  38.1 5.1 %collective-permute-done.3 = bf16[1024,128]{1,0:T(8,128)(2,1)S(1)} collective-permute-done((bf16[1024,128]{1,0:T(8,128)(2,1)}, bf16[1024,128]{1,0:T(8,128)(2,1)S(1)}, u32[]{:S(2)}, u32[]{:S(2)}) %collective-permute-start.3) | collective-permute-done | bytes 262176 | tf_op jit(solution)/shard_map/ppermute | solution.py:71
  43.2 0.5 collective-permute-start.10
  43.7 0.6 collective-permute-start.9
  44.3 1.7 %collective-permute-done.4 = bf16[1040,128]{1,0:T(8,128)(2,1)S(1)} collective-permute-done((bf16[1040,128]{1,0:T(8,128)(2,1)S(1)}, bf16[1040,128]{1,0:T(8,128)(2,1)S(1)}, u32[]{:S(2)}, u32[]{:S(2)}) %collective-permute-start.4) | collective-permute-done | bytes 266272 | tf_op jit(solution)/shard_map/ppermute | solution.py:71
  46.5 0.6 collective-permute-start.5
  47.6 0.4 copy-done
  48.0 3.5 %own_block.1 = (f32[16,128,128]{2,1,0:T(8,128)S(1)}, f32[16,128,128]{2,1,0:T(8,128)S(1)}) custom-call(s32[4,128]{1,0:T(4,128)S(1)} %pad_add_fusion.3.table, bf16[2064,128]{1,0:T(8,128)(2,1)S(1)} %pad_maximum_fusion.refs_0_, bf16[2064,128]{1,0:T(8,128)(2,1)S(1)} %collective-permute-done.refs_1_, ...), custom_call_target="tpu_custom_call" | custom-call | flops 2147483648 | bytes 2097152 | tf_op jit(solution)/shard_map/own_block/pallas_call | solution.py:253
  51.6 0.6 collective-permute-start.6
  52.6 7.1 %near_blocks.1 = (f32[16,128,128]{2,1,0:T(8,128)S(1)}, f32[16,128,128]{2,1,0:T(8,128)S(1)}) custom-call(s32[6,128]{1,0:T(8,128)S(1)} %pad_add_fusion.1.table, bf16[2064,128]{1,0:T(8,128)(2,1)S(1)} %pad_maximum_fusion.refs_0_, bf16[2064,128]{1,0:T(8,128)(2,1)S(1)} %collective-permute-done.refs_1_, ...), custom_call_target="tpu_custom_call" | custom-call | flops 4294967296 | bytes 4194304 | tf_op jit(solution)/shard_map/near_blocks/pallas_call | solution.py:253
  59.9 5.1 %help_neighbours.1 = (f32[2,16,64,128]{3,2,1,0:T(8,128)S(1)}, f32[2,16,64,128]{3,2,1,0:T(8,128)S(1)}) custom-call(s32[5,128]{1,0:T(8,128)S(1)} %fusion.4.table, bf16[64,128,128]{2,1,0:T(8,128)(2,1)} %collective-permute-done.8.refs_7_.b_y, bf16[64,128,128]{2,1,0:T(8,128)(2,1)S(1)} %collective-permute-done.7.refs_6_.b_x, ...), custom_call_target="tpu_custom_call" | custom-call | flops 2147483648 | bytes 4194304 | tf_op jit(solution)/shard_map/help_neighbours/pallas_call | solution.py:253
  65.0 0.5 collective-permute-start.11
  65.5 2.1 %collective-permute-done.12.other = f32[2,16,64,128]{3,2,1,0:T(8,128)S(1)} collective-permute-done((f32[2,16,64,128]{3,2,1,0:T(8,128)S(1)}, f32[2,16,64,128]{3,2,1,0:T(8,128)S(1)}, u32[]{:S(2)}, u32[]{:S(2)}) %collective-permute-start.12) | collective-permute-done | bytes 1048608 | tf_op jit(solution)/shard_map/ppermute | solution.py:71
  67.7 0.3 encode.1
  68.0 1.2 %collective-permute-start.13 = (s16[1040,128]{1,0:T(8,128)(2,1)S(1)}, s16[1040,128]{1,0:T(8,128)(2,1)S(1)}, u32[]{:S(2)}, u32[]{:S(2)}) collective-permute-start(s16[1040,128]{1,0:T(8,128)(2,1)S(1)} %get-tuple-element.47), channel_id=1, source_target_pairs={{0,8},{8,0},{16,24},{24,16},{1,9},{9,1},{17,25},{25,17},{2,10},{10... | collective-permute-start | bytes 798728 | tf_op jit(solution)/shard_map/ppermute | solution.py:71
  69.1 1.5 %collective-permute-start.14 = (s16[1040,128]{1,0:T(8,128)(2,1)S(1)}, s16[1040,128]{1,0:T(8,128)(2,1)S(1)}, u32[]{:S(2)}, u32[]{:S(2)}) collective-permute-start(s16[1040,128]{1,0:T(8,128)(2,1)S(1)} %get-tuple-element.48), channel_id=1, source_target_pairs={{0,16},{8,24},{16,0},{24,8},{1,17},{9,25},{17,1},{25,9},{2,18},{10... | collective-permute-start | bytes 798728 | tf_op jit(solution)/shard_map/ppermute | solution.py:71
  70.8 5.7 %collective-permute-done.13.from_x = s16[1040,128]{1,0:T(8,128)(2,1)S(1)} collective-permute-done((s16[1040,128]{1,0:T(8,128)(2,1)S(1)}, s16[1040,128]{1,0:T(8,128)(2,1)S(1)}, u32[]{:S(2)}, u32[]{:S(2)}) %collective-permute-start.13) | collective-permute-done | bytes 266272 | tf_op jit(solution)/shard_map/ppermute | solution.py:71
  76.5 0.8 %collective-permute-done.14.from_y = s16[1040,128]{1,0:T(8,128)(2,1)S(1)} collective-permute-done((s16[1040,128]{1,0:T(8,128)(2,1)S(1)}, s16[1040,128]{1,0:T(8,128)(2,1)S(1)}, u32[]{:S(2)}, u32[]{:S(2)}) %collective-permute-start.14) | collective-permute-done | bytes 266272 | tf_op jit(solution)/shard_map/ppermute | solution.py:71
  77.3 0.9 %finish.1 = bf16[16,128,128]{2,1,0:T(8,128)(2,1)} custom-call(f32[16,128,128]{2,1,0:T(8,128)S(1)} %add.59.mine, s16[1040,128]{1,0:T(8,128)(2,1)S(1)} %collective-permute-done.13.from_x, s16[1040,128]{1,0:T(8,128)(2,1)S(1)} %collective-permute-done.14.from_y), custom_call_target="tpu_custom_call" | custom-call | tf_op jit(solution)/shard_map/finish/pallas_call | solution.py:348
  (64 shorter events, 2.2 us)
Async XLA Ops:
  0.0 8.6 %copy-start.1 = (bf16[1,1,1,16,128,128]{5,4,3,2,1,0:T(8,128)(2,1)S(1)}, bf16[1,1,1,16,128,128]{5,4,3,2,1,0:T(8,128)(2,1)}, u32[]{:S(2)}) copy-start(bf16[1,1,1,16,128,128]{5,4,3,2,1,0:T(8,128)(2,1)} %param.7) | copy-start | bytes 1572868
  0.0 52.2 %collective-permute-start.7 = (bf16[64,128,128]{2,1,0:T(8,128)(2,1)}, bf16[64,128,128]{2,1,0:T(8,128)(2,1)S(1)}, u32[]{:S(2)}, u32[]{:S(2)}) collective-permute-start(bf16[64,128,128]{2,1,0:T(8,128)(2,1)} %bitcast.31), channel_id=1, source_target_pairs={{0,8},{8,0},{16,24},{24,16},{1,9},{9,1},{17,25},{25,17},{2,10},{10... | collective-permute-start | bytes 6291464 | tf_op jit(solution)/shard_map/ppermute | solution.py:71
  2.9 49.2 %collective-permute-start.8 = (bf16[64,128,128]{2,1,0:T(8,128)(2,1)}, bf16[64,128,128]{2,1,0:T(8,128)(2,1)}, u32[]{:S(2)}, u32[]{:S(2)}) collective-permute-start(bf16[64,128,128]{2,1,0:T(8,128)(2,1)} %bitcast.32), channel_id=1, source_target_pairs={{0,16},{8,24},{16,0},{24,8},{1,17},{9,25},{17,1},{25,9},{2,18},{10... | collective-permute-start | bytes 6291464 | tf_op jit(solution)/shard_map/ppermute | solution.py:71
  5.9 7.8 %copy-start.3 = (s32[1,1,32]{2,1,0:T(1,128)S(1)}, s32[1,1,32]{2,1,0:T(1,128)}, u32[]{:S(2)}) copy-start(s32[1,1,32]{2,1,0:T(1,128)} %param.13) | copy-start | bytes 388
  5.9 7.8 %copy-start.4 = (s32[1,1,1,64]{3,2,1,0:T(1,128)S(1)}, s32[1,1,1,64]{3,2,1,0:T(1,128)}, u32[]{:S(2)}) copy-start(s32[1,1,1,64]{3,2,1,0:T(1,128)} %param.11) | copy-start | bytes 772
  7.0 36.8 %collective-permute-start = (bf16[2064,128]{1,0:T(8,128)(2,1)S(1)}, bf16[2064,128]{1,0:T(8,128)(2,1)S(1)}, u32[]{:S(2)}, u32[]{:S(2)}) collective-permute-start(bf16[2064,128]{1,0:T(8,128)(2,1)S(1)} %pad_maximum_fusion.refs_0_), channel_id=1, source_target_pairs={{0,2},{2,0},{4,6},{6,4},{1,3},{3,1},{5,7},{7,5},{8,10},{10,8},{12,... | collective-permute-start | bytes 1585160 | tf_op jit(solution)/shard_map/ppermute | solution.py:71
  9.3 26.6 %collective-permute-start.2 = (bf16[1040,128]{1,0:T(8,128)(2,1)}, bf16[1040,128]{1,0:T(8,128)(2,1)S(1)}, u32[]{:S(2)}, u32[]{:S(2)}) collective-permute-start(bf16[1040,128]{1,0:T(8,128)(2,1)} %fusion), channel_id=1, source_target_pairs={{0,4},{2,6},{4,0},{6,2},{1,5},{3,7},{5,1},{7,3},{8,12},{10,14},{12... | collective-permute-start | bytes 798728 | tf_op jit(solution)/shard_map/ppermute | solution.py:71
  12.6 22.3 %collective-permute-start.1 = (bf16[1024,128]{1,0:T(8,128)(2,1)}, bf16[1024,128]{1,0:T(8,128)(2,1)}, u32[]{:S(2)}, u32[]{:S(2)}) collective-permute-start(bf16[1024,128]{1,0:T(8,128)(2,1)} %bitcast.3), channel_id=1, source_target_pairs={{0,4},{2,6},{4,0},{6,2},{1,5},{3,7},{5,1},{7,3},{8,12},{10,14},{12... | collective-permute-start | bytes 786440 | tf_op jit(solution)/shard_map/ppermute | solution.py:71
  15.3 30.8 %copy-start.2 = (bf16[1,1,1,16,128,128]{5,4,3,2,1,0:T(8,128)(2,1)S(1)}, bf16[1,1,1,16,128,128]{5,4,3,2,1,0:T(8,128)(2,1)}, u32[]{:S(2)}) copy-start(bf16[1,1,1,16,128,128]{5,4,3,2,1,0:T(8,128)(2,1)} %param.7) | copy-start | bytes 1572868
  34.9 8.3 %collective-permute-start.3 = (bf16[1024,128]{1,0:T(8,128)(2,1)}, bf16[1024,128]{1,0:T(8,128)(2,1)S(1)}, u32[]{:S(2)}, u32[]{:S(2)}) collective-permute-start(bf16[1024,128]{1,0:T(8,128)(2,1)} %collective-permute-done.1), channel_id=1, source_target_pairs={{0,2},{2,0},{4,6},{6,4},{1,3},{3,1},{5,7},{7,5},{8,10},{10,8},{12,... | collective-permute-start | bytes 786440 | tf_op jit(solution)/shard_map/ppermute | solution.py:71
  36.0 10.1 %collective-permute-start.4 = (bf16[1040,128]{1,0:T(8,128)(2,1)S(1)}, bf16[1040,128]{1,0:T(8,128)(2,1)S(1)}, u32[]{:S(2)}, u32[]{:S(2)}) collective-permute-start(bf16[1040,128]{1,0:T(8,128)(2,1)S(1)} %collective-permute-done.2), channel_id=1, source_target_pairs={{0,2},{2,0},{4,6},{6,4},{1,3},{3,1},{5,7},{7,5},{8,10},{10,8},{12,... | collective-permute-start | bytes 798728 | tf_op jit(solution)/shard_map/ppermute | solution.py:71
  43.2 8.4 %collective-permute-start.10 = (s32[97]{0:T(128)S(1)}, s32[97]{0:T(128)S(1)}, u32[]{:S(2)}, u32[]{:S(2)}) collective-permute-start(s32[97]{0:T(128)S(1)} %pad_add_fusion.5), channel_id=1, source_target_pairs={{0,16},{8,24},{16,0},{24,8},{1,17},{9,25},{17,1},{25,9},{2,18},{10... | collective-permute-start | bytes 1172 | tf_op jit(solution)/shard_map/ppermute | solution.py:71
  43.7 8.4 %collective-permute-start.9 = (s32[97]{0:T(128)S(1)}, s32[97]{0:T(128)S(1)}, u32[]{:S(2)}, u32[]{:S(2)}) collective-permute-start(s32[97]{0:T(128)S(1)} %pad_add_fusion.5), channel_id=1, source_target_pairs={{0,8},{8,0},{16,24},{24,16},{1,9},{9,1},{17,25},{25,17},{2,10},{10... | collective-permute-start | bytes 1172 | tf_op jit(solution)/shard_map/ppermute | solution.py:71
  46.4 1.6 %copy-start = (bf16[1,1,1,64,128,128]{5,4,3,2,1,0:T(8,128)(2,1)S(1)}, bf16[1,1,1,64,128,128]{5,4,3,2,1,0:T(8,128)(2,1)}, u32[]{:S(2)}) copy-start(bf16[1,1,1,64,128,128]{5,4,3,2,1,0:T(8,128)(2,1)} %param.10) | copy-start | bytes 6291460
  46.5 13.3 %collective-permute-start.5 = (bf16[1040,128]{1,0:T(8,128)(2,1)S(1)}, bf16[1040,128]{1,0:T(8,128)(2,1)S(1)}, u32[]{:S(2)}, u32[]{:S(2)}) collective-permute-start(bf16[1040,128]{1,0:T(8,128)(2,1)S(1)} %get-tuple-element.52), channel_id=1, source_target_pairs={{0,8},{8,0},{16,24},{24,16},{1,9},{9,1},{17,25},{25,17},{2,10},{10... | collective-permute-start | bytes 798728 | tf_op jit(solution)/shard_map/ppermute | solution.py:71
  51.6 8.2 %collective-permute-start.6 = (bf16[1040,128]{1,0:T(8,128)(2,1)S(1)}, bf16[1040,128]{1,0:T(8,128)(2,1)S(1)}, u32[]{:S(2)}, u32[]{:S(2)}) collective-permute-start(bf16[1040,128]{1,0:T(8,128)(2,1)S(1)} %get-tuple-element.51), channel_id=1, source_target_pairs={{0,16},{8,24},{16,0},{24,8},{1,17},{9,25},{17,1},{25,9},{2,18},{10... | collective-permute-start | bytes 798728 | tf_op jit(solution)/shard_map/ppermute | solution.py:71
  64.9 2.7 %collective-permute-start.12 = (f32[2,16,64,128]{3,2,1,0:T(8,128)S(1)}, f32[2,16,64,128]{3,2,1,0:T(8,128)S(1)}, u32[]{:S(2)}, u32[]{:S(2)}) collective-permute-start(f32[2,16,64,128]{3,2,1,0:T(8,128)S(1)} %get-tuple-element.46), channel_id=1, source_target_pairs={{0,1},{1,0},{2,3},{3,2},{4,5},{5,4},{6,7},{7,6},{8,9},{9,8},{10,11... | collective-permute-start | bytes 3145736 | tf_op jit(solution)/shard_map/ppermute | solution.py:71
  65.0 5.6 %collective-permute-start.11 = (f32[16,128,128]{2,1,0:T(8,128)S(1)}, f32[16,128,128]{2,1,0:T(8,128)S(1)}, u32[]{:S(2)}, u32[]{:S(2)}) collective-permute-start(f32[16,128,128]{2,1,0:T(8,128)S(1)} %get-tuple-element.42), channel_id=1, source_target_pairs={{0,1},{1,0},{2,3},{3,2},{4,5},{5,4},{6,7},{7,6},{8,9},{9,8},{10,11... | collective-permute-start | bytes 3145736 | tf_op jit(solution)/shard_map/ppermute | solution.py:71
  68.0 8.5 %collective-permute-start.13 = (s16[1040,128]{1,0:T(8,128)(2,1)S(1)}, s16[1040,128]{1,0:T(8,128)(2,1)S(1)}, u32[]{:S(2)}, u32[]{:S(2)}) collective-permute-start(s16[1040,128]{1,0:T(8,128)(2,1)S(1)} %get-tuple-element.47), channel_id=1, source_target_pairs={{0,8},{8,0},{16,24},{24,16},{1,9},{9,1},{17,25},{25,17},{2,10},{10... | collective-permute-start | bytes 798728 | tf_op jit(solution)/shard_map/ppermute | solution.py:71
  69.1 8.2 %collective-permute-start.14 = (s16[1040,128]{1,0:T(8,128)(2,1)S(1)}, s16[1040,128]{1,0:T(8,128)(2,1)S(1)}, u32[]{:S(2)}, u32[]{:S(2)}) collective-permute-start(s16[1040,128]{1,0:T(8,128)(2,1)S(1)} %get-tuple-element.48), channel_id=1, source_target_pairs={{0,16},{8,24},{16,0},{24,8},{1,17},{9,25},{17,1},{25,9},{2,18},{10... | collective-permute-start | bytes 798728 | tf_op jit(solution)/shard_map/ppermute | solution.py:71

commit v4 on v3

--- a/solution.py
+++ b/solution.py
@@ -303,13 +303,13 @@
     part_keep, part_give = call(
         help_neighbours, "help_neighbours", table, (), (b_y, b_x), part, low, (2,), (upper, lower)
     )
-    part_other = swap_layers(part_give)
+    part_other = [swap_layers(part_give[q]) for q in range(2)]
     other = swap_layers(give)
     steps = half * low
 
-    def encode(keep, other, *codes):
-        for q, code in enumerate(codes):
-            values = [keep[q, o] + other[q, o] for o in range(half)]
+    def encode(q):
+        def kernel(keep, other, code):
+            values = [keep[q, o] + other[o] for o in range(half)]
             tops = [jnp.max(jnp.abs(v), axis=0, keepdims=True) for v in values]
             top = jnp.maximum(jnp.concatenate(tops, axis=0), 1e-30)
             exponent = jnp.ceil(jnp.log2(top))
@@ -319,6 +319,8 @@
                 value = jnp.round(value).astype(jnp.int32)
                 code[o * low : (o + 1) * low, :] = value.astype(jnp.int16)
             code[steps:, :] = exponent.astype(jnp.int32).astype(jnp.int16)
+
+        return kernel
 
     def finish(mine, from_x, from_y, out, rounded, sems):
         codes = (from_x, from_y)
@@ -339,10 +341,17 @@
             c.wait()
 
     code = jax.ShapeDtypeStruct((steps + half, side), jnp.int16)
-    code_x, code_y = pl.pallas_call(
-        encode, in_specs=[vmem] * 2, out_specs=(vmem, vmem), out_shape=(code, code), name="encode",
-        compiler_params=pltpu.CompilerParams(vmem_limit_bytes=10 * 2**20),
-    )(part_keep, part_other)
+    code_x, code_y = (
+        pl.pallas_call(
+            encode(q),
+            in_specs=[vmem] * 2,
+            out_specs=vmem,
+            out_shape=code,
+            compiler_params=pltpu.CompilerParams(vmem_limit_bytes=10 * 2**20),
+            name=name,
+        )(part_keep, part_other[q])
+        for q, name in enumerate(("encode_x", "encode_y"))
+    )
     from_x, from_y = flip(code_x, 1), flip(code_y, 2)
     mine = keep + other
     result = pl.pallas_call(

time: 78.6 us -> 78.9 us (level)
    ppermute x15 -> x16, starting transfers between devices: 16.6 us -> 16.8 us  [across(): return lax.ppermute(x, axes, pairs)]
    ppermute x15 -> x16, waiting for transfers between devices: 35.1 us -> 34.9 us  [across(): return lax.ppermute(x, axes, pairs)]
  transfers between devices with their start and end apart: 15 -> 16, of which waited for: 6 -> 6; matrix products, arithmetic and copies ran while one was open for 10% -> 10% of each run, Pallas kernels for 14% -> 20%
where the time goes in v4:
time: 78.9 us; the launch traced here: 78.6 us
  waiting for transfers between devices  34.9 us (44%)
  Pallas kernels  16.9 us (21%)
  starting transfers between devices  16.8 us (21%)
  other arithmetic  4.48 us (6%)
  local copies, waits for them, and re-layouts  3.64 us (5%)
  between operations  1.78 us (2%)
    ppermute x16, waiting for transfers between devices, across(): return lax.ppermute(x, axes, pairs)  34.9 us
    ppermute x16, starting transfers between devices, across(): return lax.ppermute(x, axes, pairs)  16.8 us
    pallas_call x3, Pallas kernels, call(): pl.pallas_call(kernel, in_specs=[smem] + [vmem] * len(near) + [hbm] * len...  15.7 us
    concatenate x2, other arithmetic, planned_shards(): a = jnp.concatenate([a_tiles.reshape(na * side, side), a_note])  1.83 us
  transfers between devices with their start and end apart: 16, of which 6 were waited for; matrix products, arithmetic and copies ran while one was open for 10% of the time, Pallas kernels for 20%

profile of v4, /device:TPU:0, one launch (start us, length us, event | category | flops | bytes accessed | tf_op | source)
XLA Modules:
  0.0 78.6 jit_solution(17576180619159173886)
XLA Ops:
  0.0 2.9 %collective-permute-start.7 = (bf16[64,128,128]{2,1,0:T(8,128)(2,1)}, bf16[64,128,128]{2,1,0:T(8,128)(2,1)S(1)}, u32[]{:S(2)}, u32[]{:S(2)}) collective-permute-start(bf16[64,128,128]{2,1,0:T(8,128)(2,1)} %bitcast.35), channel_id=1, source_target_pairs={{0,8},{8,0},{16,24},{24,16},{1,9},{9,1},{17,25},{25,17},{2,10},{10... | collective-permute-start | bytes 6291464 | tf_op jit(solution)/shard_map/ppermute | solution.py:71
  2.9 1.5 %collective-permute-start.8 = (bf16[64,128,128]{2,1,0:T(8,128)(2,1)}, bf16[64,128,128]{2,1,0:T(8,128)(2,1)}, u32[]{:S(2)}, u32[]{:S(2)}) collective-permute-start(bf16[64,128,128]{2,1,0:T(8,128)(2,1)} %bitcast.36), channel_id=1, source_target_pairs={{0,16},{8,24},{16,0},{24,8},{1,17},{9,25},{17,1},{25,9},{2,18},{10... | collective-permute-start | bytes 6291464 | tf_op jit(solution)/shard_map/ppermute | solution.py:71
  5.1 0.7 convert_bitcast_fusion
  5.9 1.1 %pad_maximum_fusion.refs_0_ = bf16[2064,128]{1,0:T(8,128)(2,1)S(1)} fusion(bf16[16,128]{1,0:T(8,128)(2,1)S(1)} %broadcast_in_dim.65, bf16[2048,128]{1,0:T(8,128)(2,1)} %bitcast.38), kind=kLoop, calls=%fused_computation.1 | loop fusion | flops 1056768 | bytes 1056768 | tf_op jit(solution)/shard_map/concatenate | solution.py:152
  7.0 1.6 %collective-permute-start = (bf16[2064,128]{1,0:T(8,128)(2,1)S(1)}, bf16[2064,128]{1,0:T(8,128)(2,1)S(1)}, u32[]{:S(2)}, u32[]{:S(2)}) collective-permute-start(bf16[2064,128]{1,0:T(8,128)(2,1)S(1)} %pad_maximum_fusion.refs_0_), channel_id=1, source_target_pairs={{0,2},{2,0},{4,6},{6,4},{1,3},{3,1},{5,7},{7,5},{8,10},{10,8},{12,... | collective-permute-start | bytes 1585160 | tf_op jit(solution)/shard_map/ppermute | solution.py:71
  8.6 0.7 fusion
  9.3 2.6 %collective-permute-start.2 = (bf16[1040,128]{1,0:T(8,128)(2,1)}, bf16[1040,128]{1,0:T(8,128)(2,1)S(1)}, u32[]{:S(2)}, u32[]{:S(2)}) collective-permute-start(bf16[1040,128]{1,0:T(8,128)(2,1)} %fusion), channel_id=1, source_target_pairs={{0,4},{2,6},{4,0},{6,2},{1,5},{3,7},{5,1},{7,3},{8,12},{10,14},{12... | collective-permute-start | bytes 798728 | tf_op jit(solution)/shard_map/ppermute | solution.py:71
  11.9 0.7 slice.80
  12.7 0.3 collective-permute-start.1
  13.7 0.6 slice.97
  14.4 0.7 iota_compare_fusion.5
  15.5 19.5 %collective-permute-done.1 = bf16[1024,128]{1,0:T(8,128)(2,1)} collective-permute-done((bf16[1024,128]{1,0:T(8,128)(2,1)}, bf16[1024,128]{1,0:T(8,128)(2,1)}, u32[]{:S(2)}, u32[]{:S(2)}) %collective-permute-start.1) | collective-permute-done | bytes 262176 | tf_op jit(solution)/shard_map/ppermute | solution.py:71
  34.9 1.0 %constant_dynamic-update-slice_fusion.1 = bf16[2064,128]{1,0:T(8,128)(2,1)S(1)} fusion(bf16[1024,128]{1,0:T(8,128)(2,1)} %collective-permute-done.1), kind=kLoop, calls=%fused_computation.19 | loop fusion | bytes 524288
  36.0 2.1 %collective-permute-start.4 = (bf16[1040,128]{1,0:T(8,128)(2,1)S(1)}, bf16[1040,128]{1,0:T(8,128)(2,1)S(1)}, u32[]{:S(2)}, u32[]{:S(2)}) collective-permute-start(bf16[1040,128]{1,0:T(8,128)(2,1)S(1)} %collective-permute-done.2), channel_id=1, source_target_pairs={{0,2},{2,0},{4,6},{6,4},{1,3},{3,1},{5,7},{7,5},{8,10},{10,8},{12,... | collective-permute-start | bytes 798728 | tf_op jit(solution)/shard_map/ppermute | solution.py:71
  38.1 5.1 %collective-permute-done.3 = bf16[1024,128]{1,0:T(8,128)(2,1)S(1)} collective-permute-done((bf16[1024,128]{1,0:T(8,128)(2,1)}, bf16[1024,128]{1,0:T(8,128)(2,1)S(1)}, u32[]{:S(2)}, u32[]{:S(2)}) %collective-permute-start.3) | collective-permute-done | bytes 262176 | tf_op jit(solution)/shard_map/ppermute | solution.py:71
  43.2 0.5 collective-permute-start.10
  43.7 0.6 collective-permute-start.9
  44.3 1.7 %collective-permute-done.4 = bf16[1040,128]{1,0:T(8,128)(2,1)S(1)} collective-permute-done((bf16[1040,128]{1,0:T(8,128)(2,1)S(1)}, bf16[1040,128]{1,0:T(8,128)(2,1)S(1)}, u32[]{:S(2)}, u32[]{:S(2)}) %collective-permute-start.4) | collective-permute-done | bytes 266272 | tf_op jit(solution)/shard_map/ppermute | solution.py:71
  46.1 0.3 select_select_fusion
  46.5 0.6 collective-permute-start.5
  47.6 0.4 copy-done
  48.0 3.5 %own_block.1 = (f32[16,128,128]{2,1,0:T(8,128)S(1)}, f32[16,128,128]{2,1,0:T(8,128)S(1)}) custom-call(s32[4,128]{1,0:T(4,128)S(1)} %pad_add_fusion.3.table, bf16[2064,128]{1,0:T(8,128)(2,1)S(1)} %pad_maximum_fusion.refs_0_, bf16[2064,128]{1,0:T(8,128)(2,1)S(1)} %collective-permute-done.refs_1_, ...), custom_call_target="tpu_custom_call" | custom-call | flops 2147483648 | bytes 2097152 | tf_op jit(solution)/shard_map/own_block/pallas_call | solution.py:253
  51.6 0.6 collective-permute-start.6
  52.6 7.1 %near_blocks.1 = (f32[16,128,128]{2,1,0:T(8,128)S(1)}, f32[16,128,128]{2,1,0:T(8,128)S(1)}) custom-call(s32[6,128]{1,0:T(8,128)S(1)} %pad_add_fusion.1.table, bf16[2064,128]{1,0:T(8,128)(2,1)S(1)} %pad_maximum_fusion.refs_0_, bf16[2064,128]{1,0:T(8,128)(2,1)S(1)} %collective-permute-done.refs_1_, ...), custom_call_target="tpu_custom_call" | custom-call | flops 4294967296 | bytes 4194304 | tf_op jit(solution)/shard_map/near_blocks/pallas_call | solution.py:253
  59.9 5.1 %help_neighbours.1 = (f32[2,16,64,128]{3,2,1,0:T(8,128)S(1)}, f32[2,16,64,128]{3,2,1,0:T(8,128)S(1)}) custom-call(s32[5,128]{1,0:T(8,128)S(1)} %fusion.4.table, bf16[64,128,128]{2,1,0:T(8,128)(2,1)} %collective-permute-done.8.refs_7_.b_y, bf16[64,128,128]{2,1,0:T(8,128)(2,1)S(1)} %collective-permute-done.7.refs_6_.b_x, ...), custom_call_target="tpu_custom_call" | custom-call | flops 2147483648 | bytes 4194304 | tf_op jit(solution)/shard_map/help_neighbours/pallas_call | solution.py:253
  65.1 0.6 collective-permute-start.14
  65.7 1.5 %collective-permute-done.14.other = f32[16,64,128]{2,1,0:T(8,128)S(1)} collective-permute-done((f32[16,64,128]{2,1,0:T(8,128)S(1)}, f32[16,64,128]{2,1,0:T(8,128)S(1)}, u32[]{:S(2)}, u32[]{:S(2)}) %collective-permute-start.14) | collective-permute-done | bytes 524320 | tf_op jit(solution)/shard_map/ppermute | solution.py:71
  67.4 1.6 %collective-permute-start.15 = (s16[1040,128]{1,0:T(8,128)(2,1)S(1)}, s16[1040,128]{1,0:T(8,128)(2,1)S(1)}, u32[]{:S(2)}, u32[]{:S(2)}) collective-permute-start(s16[1040,128]{1,0:T(8,128)(2,1)S(1)} %encode_y.1), channel_id=1, source_target_pairs={{0,16},{8,24},{16,0},{24,8},{1,17},{9,25},{17,1},{25,9},{2,18},{10... | collective-permute-start | bytes 798728 | tf_op jit(solution)/shard_map/ppermute | solution.py:71
  69.1 1.1 %collective-permute-start.13 = (s16[1040,128]{1,0:T(8,128)(2,1)S(1)}, s16[1040,128]{1,0:T(8,128)(2,1)S(1)}, u32[]{:S(2)}, u32[]{:S(2)}) collective-permute-start(s16[1040,128]{1,0:T(8,128)(2,1)S(1)} %encode_x.1), channel_id=1, source_target_pairs={{0,8},{8,0},{16,24},{24,16},{1,9},{9,1},{17,25},{25,17},{2,10},{10... | collective-permute-start | bytes 798728 | tf_op jit(solution)/shard_map/ppermute | solution.py:71
  70.4 5.7 %collective-permute-done.15.from_y = s16[1040,128]{1,0:T(8,128)(2,1)S(1)} collective-permute-done((s16[1040,128]{1,0:T(8,128)(2,1)S(1)}, s16[1040,128]{1,0:T(8,128)(2,1)S(1)}, u32[]{:S(2)}, u32[]{:S(2)}) %collective-permute-start.15) | collective-permute-done | bytes 266272 | tf_op jit(solution)/shard_map/ppermute | solution.py:71
  76.1 1.5 %collective-permute-done.13.from_x = s16[1040,128]{1,0:T(8,128)(2,1)S(1)} collective-permute-done((s16[1040,128]{1,0:T(8,128)(2,1)S(1)}, s16[1040,128]{1,0:T(8,128)(2,1)S(1)}, u32[]{:S(2)}, u32[]{:S(2)}) %collective-permute-start.13) | collective-permute-done | bytes 266272 | tf_op jit(solution)/shard_map/ppermute | solution.py:71
  77.6 0.9 %finish.1 = bf16[16,128,128]{2,1,0:T(8,128)(2,1)} custom-call(f32[16,128,128]{2,1,0:T(8,128)S(1)} %add.59.mine, s16[1040,128]{1,0:T(8,128)(2,1)S(1)} %collective-permute-done.13.from_x, s16[1040,128]{1,0:T(8,128)(2,1)S(1)} %collective-permute-done.15.from_y), custom_call_target="tpu_custom_call" | custom-call | tf_op jit(solution)/shard_map/finish/pallas_call | solution.py:357
  (68 shorter events, 2.4 us)
Async XLA Ops:
  0.0 8.6 %copy-start.1 = (bf16[1,1,1,16,128,128]{5,4,3,2,1,0:T(8,128)(2,1)S(1)}, bf16[1,1,1,16,128,128]{5,4,3,2,1,0:T(8,128)(2,1)}, u32[]{:S(2)}) copy-start(bf16[1,1,1,16,128,128]{5,4,3,2,1,0:T(8,128)(2,1)} %param.7) | copy-start | bytes 1572868
  0.0 52.2 %collective-permute-start.7 = (bf16[64,128,128]{2,1,0:T(8,128)(2,1)}, bf16[64,128,128]{2,1,0:T(8,128)(2,1)S(1)}, u32[]{:S(2)}, u32[]{:S(2)}) collective-permute-start(bf16[64,128,128]{2,1,0:T(8,128)(2,1)} %bitcast.35), channel_id=1, source_target_pairs={{0,8},{8,0},{16,24},{24,16},{1,9},{9,1},{17,25},{25,17},{2,10},{10... | collective-permute-start | bytes 6291464 | tf_op jit(solution)/shard_map/ppermute | solution.py:71
  2.9 49.2 %collective-permute-start.8 = (bf16[64,128,128]{2,1,0:T(8,128)(2,1)}, bf16[64,128,128]{2,1,0:T(8,128)(2,1)}, u32[]{:S(2)}, u32[]{:S(2)}) collective-permute-start(bf16[64,128,128]{2,1,0:T(8,128)(2,1)} %bitcast.36), channel_id=1, source_target_pairs={{0,16},{8,24},{16,0},{24,8},{1,17},{9,25},{17,1},{25,9},{2,18},{10... | collective-permute-start | bytes 6291464 | tf_op jit(solution)/shard_map/ppermute | solution.py:71
  5.9 7.8 %copy-start.3 = (s32[1,1,32]{2,1,0:T(1,128)S(1)}, s32[1,1,32]{2,1,0:T(1,128)}, u32[]{:S(2)}) copy-start(s32[1,1,32]{2,1,0:T(1,128)} %param.13) | copy-start | bytes 388
  5.9 7.8 %copy-start.4 = (s32[1,1,1,64]{3,2,1,0:T(1,128)S(1)}, s32[1,1,1,64]{3,2,1,0:T(1,128)}, u32[]{:S(2)}) copy-start(s32[1,1,1,64]{3,2,1,0:T(1,128)} %param.11) | copy-start | bytes 772
  7.0 36.8 %collective-permute-start = (bf16[2064,128]{1,0:T(8,128)(2,1)S(1)}, bf16[2064,128]{1,0:T(8,128)(2,1)S(1)}, u32[]{:S(2)}, u32[]{:S(2)}) collective-permute-start(bf16[2064,128]{1,0:T(8,128)(2,1)S(1)} %pad_maximum_fusion.refs_0_), channel_id=1, source_target_pairs={{0,2},{2,0},{4,6},{6,4},{1,3},{3,1},{5,7},{7,5},{8,10},{10,8},{12,... | collective-permute-start | bytes 1585160 | tf_op jit(solution)/shard_map/ppermute | solution.py:71
  9.3 26.6 %collective-permute-start.2 = (bf16[1040,128]{1,0:T(8,128)(2,1)}, bf16[1040,128]{1,0:T(8,128)(2,1)S(1)}, u32[]{:S(2)}, u32[]{:S(2)}) collective-permute-start(bf16[1040,128]{1,0:T(8,128)(2,1)} %fusion), channel_id=1, source_target_pairs={{0,4},{2,6},{4,0},{6,2},{1,5},{3,7},{5,1},{7,3},{8,12},{10,14},{12... | collective-permute-start | bytes 798728 | tf_op jit(solution)/shard_map/ppermute | solution.py:71
  12.7 22.3 %collective-permute-start.1 = (bf16[1024,128]{1,0:T(8,128)(2,1)}, bf16[1024,128]{1,0:T(8,128)(2,1)}, u32[]{:S(2)}, u32[]{:S(2)}) collective-permute-start(bf16[1024,128]{1,0:T(8,128)(2,1)} %bitcast.3), channel_id=1, source_target_pairs={{0,4},{2,6},{4,0},{6,2},{1,5},{3,7},{5,1},{7,3},{8,12},{10,14},{12... | collective-permute-start | bytes 786440 | tf_op jit(solution)/shard_map/ppermute | solution.py:71
  15.5 30.6 %copy-start.2 = (bf16[1,1,1,16,128,128]{5,4,3,2,1,0:T(8,128)(2,1)S(1)}, bf16[1,1,1,16,128,128]{5,4,3,2,1,0:T(8,128)(2,1)}, u32[]{:S(2)}) copy-start(bf16[1,1,1,16,128,128]{5,4,3,2,1,0:T(8,128)(2,1)} %param.7) | copy-start | bytes 1572868
  34.9 8.3 %collective-permute-start.3 = (bf16[1024,128]{1,0:T(8,128)(2,1)}, bf16[1024,128]{1,0:T(8,128)(2,1)S(1)}, u32[]{:S(2)}, u32[]{:S(2)}) collective-permute-start(bf16[1024,128]{1,0:T(8,128)(2,1)} %collective-permute-done.1), channel_id=1, source_target_pairs={{0,2},{2,0},{4,6},{6,4},{1,3},{3,1},{5,7},{7,5},{8,10},{10,8},{12,... | collective-permute-start | bytes 786440 | tf_op jit(solution)/shard_map/ppermute | solution.py:71
  36.0 10.1 %collective-permute-start.4 = (bf16[1040,128]{1,0:T(8,128)(2,1)S(1)}, bf16[1040,128]{1,0:T(8,128)(2,1)S(1)}, u32[]{:S(2)}, u32[]{:S(2)}) collective-permute-start(bf16[1040,128]{1,0:T(8,128)(2,1)S(1)} %collective-permute-done.2), channel_id=1, source_target_pairs={{0,2},{2,0},{4,6},{6,4},{1,3},{3,1},{5,7},{7,5},{8,10},{10,8},{12,... | collective-permute-start | bytes 798728 | tf_op jit(solution)/shard_map/ppermute | solution.py:71
  43.2 8.4 %collective-permute-start.10 = (s32[97]{0:T(128)S(1)}, s32[97]{0:T(128)S(1)}, u32[]{:S(2)}, u32[]{:S(2)}) collective-permute-start(s32[97]{0:T(128)S(1)} %pad_add_fusion.5), channel_id=1, source_target_pairs={{0,16},{8,24},{16,0},{24,8},{1,17},{9,25},{17,1},{25,9},{2,18},{10... | collective-permute-start | bytes 1172 | tf_op jit(solution)/shard_map/ppermute | solution.py:71
  43.7 8.4 %collective-permute-start.9 = (s32[97]{0:T(128)S(1)}, s32[97]{0:T(128)S(1)}, u32[]{:S(2)}, u32[]{:S(2)}) collective-permute-start(s32[97]{0:T(128)S(1)} %pad_add_fusion.5), channel_id=1, source_target_pairs={{0,8},{8,0},{16,24},{24,16},{1,9},{9,1},{17,25},{25,17},{2,10},{10... | collective-permute-start | bytes 1172 | tf_op jit(solution)/shard_map/ppermute | solution.py:71
  46.4 1.6 %copy-start = (bf16[1,1,1,64,128,128]{5,4,3,2,1,0:T(8,128)(2,1)S(1)}, bf16[1,1,1,64,128,128]{5,4,3,2,1,0:T(8,128)(2,1)}, u32[]{:S(2)}) copy-start(bf16[1,1,1,64,128,128]{5,4,3,2,1,0:T(8,128)(2,1)} %param.10) | copy-start | bytes 6291460
  46.5 13.3 %collective-permute-start.5 = (bf16[1040,128]{1,0:T(8,128)(2,1)S(1)}, bf16[1040,128]{1,0:T(8,128)(2,1)S(1)}, u32[]{:S(2)}, u32[]{:S(2)}) collective-permute-start(bf16[1040,128]{1,0:T(8,128)(2,1)S(1)} %get-tuple-element.50), channel_id=1, source_target_pairs={{0,8},{8,0},{16,24},{24,16},{1,9},{9,1},{17,25},{25,17},{2,10},{10... | collective-permute-start | bytes 798728 | tf_op jit(solution)/shard_map/ppermute | solution.py:71
  51.6 8.2 %collective-permute-start.6 = (bf16[1040,128]{1,0:T(8,128)(2,1)S(1)}, bf16[1040,128]{1,0:T(8,128)(2,1)S(1)}, u32[]{:S(2)}, u32[]{:S(2)}) collective-permute-start(bf16[1040,128]{1,0:T(8,128)(2,1)S(1)} %get-tuple-element.49), channel_id=1, source_target_pairs={{0,16},{8,24},{16,0},{24,8},{1,17},{9,25},{17,1},{25,9},{2,18},{10... | collective-permute-start | bytes 798728 | tf_op jit(solution)/shard_map/ppermute | solution.py:71
  59.8 10.4 %collective-permute-start.11 = (f32[16,128,128]{2,1,0:T(8,128)S(1)}, f32[16,128,128]{2,1,0:T(8,128)S(1)}, u32[]{:S(2)}, u32[]{:S(2)}) collective-permute-start(f32[16,128,128]{2,1,0:T(8,128)S(1)} %get-tuple-element.40), channel_id=1, source_target_pairs={{0,1},{1,0},{2,3},{3,2},{4,5},{5,4},{6,7},{7,6},{8,9},{9,8},{10,11... | collective-permute-start | bytes 3145736 | tf_op jit(solution)/shard_map/ppermute | solution.py:71
  65.1 2.1 %collective-permute-start.14 = (f32[16,64,128]{2,1,0:T(8,128)S(1)}, f32[16,64,128]{2,1,0:T(8,128)S(1)}, u32[]{:S(2)}, u32[]{:S(2)}) collective-permute-start(f32[16,64,128]{2,1,0:T(8,128)S(1)} %get-tuple-element.45), channel_id=1, source_target_pairs={{0,1},{1,0},{2,3},{3,2},{4,5},{5,4},{6,7},{7,6},{8,9},{9,8},{10,11... | collective-permute-start | bytes 1572872 | tf_op jit(solution)/shard_map/ppermute | solution.py:71
  65.7 3.3 %collective-permute-start.12 = (f32[16,64,128]{2,1,0:T(8,128)S(1)}, f32[16,64,128]{2,1,0:T(8,128)S(1)}, u32[]{:S(2)}, u32[]{:S(2)}) collective-permute-start(f32[16,64,128]{2,1,0:T(8,128)S(1)} %get-tuple-element.46), channel_id=1, source_target_pairs={{0,1},{1,0},{2,3},{3,2},{4,5},{5,4},{6,7},{7,6},{8,9},{9,8},{10,11... | collective-permute-start | bytes 1572872 | tf_op jit(solution)/shard_map/ppermute | solution.py:71
  67.4 8.7 %collective-permute-start.15 = (s16[1040,128]{1,0:T(8,128)(2,1)S(1)}, s16[1040,128]{1,0:T(8,128)(2,1)S(1)}, u32[]{:S(2)}, u32[]{:S(2)}) collective-permute-start(s16[1040,128]{1,0:T(8,128)(2,1)S(1)} %encode_y.1), channel_id=1, source_target_pairs={{0,16},{8,24},{16,0},{24,8},{1,17},{9,25},{17,1},{25,9},{2,18},{10... | collective-permute-start | bytes 798728 | tf_op jit(solution)/shard_map/ppermute | solution.py:71
  69.1 8.4 %collective-permute-start.13 = (s16[1040,128]{1,0:T(8,128)(2,1)S(1)}, s16[1040,128]{1,0:T(8,128)(2,1)S(1)}, u32[]{:S(2)}, u32[]{:S(2)}) collective-permute-start(s16[1040,128]{1,0:T(8,128)(2,1)S(1)} %encode_x.1), channel_id=1, source_target_pairs={{0,8},{8,0},{16,24},{24,16},{1,9},{9,1},{17,25},{25,17},{2,10},{10... | collective-permute-start | bytes 798728 | tf_op jit(solution)/shard_map/ppermute | solution.py:71
